TPU v7x, 256 devices: a whole 4x4x8 slice. The times are simulated.
256 devices in a mesh: gx: 8 (over x, y_lo), gy: 32 (over z, y_hi, core).
Axes of the slice: x: 4, y: 4 (y_hi: 2, y_lo: 2; y = y_hi * 2 + y_lo), z: 8, core: 2. Of those that a mesh axis runs over, the one named last changes fastest.
Arguments:
- frames: bfloat16 [65536, 1280], P(('gx', 'gy')), may hold values from -6 to 6
- lengths: int32 [256], replicated, may hold values from 1 to 256, 32768 in all
- matchings: int32 [2, 256], replicated, may hold values from 0 to 255, as said below
- wqkv: bfloat16 [2, 1280, 3840], P(None, 'gy'), may hold values from -1 to 1
- wout: bfloat16 [1, 1280, 1280], P(None, 'gy'), may hold values from -0.15625 to 0.15625
Outputs:
- stream: bfloat16 [65536, 1280], P(('gx', 'gy'))
- context: bfloat16 [65536, 1280], P(('gx', 'gy'))
Inputs may be any that keep to these rules, and one draw needn't show every extreme that they name: `matchings`: each row pairs the blocks: the partner of a block's partner is the block itself, and no block is its own partner. The lengths sum to 32768 and some block has all 256 frames valid.
All inputs are finite; a program needn't handle non-finite values.
Results may differ from a plain program's by a relative error of at most 0.029.
The roundings to bfloat16 on the way count: a program that leaves them out, or rounds other values in their place, can miss the bound.
Values may be sent and summed in bfloat16 or wider, within the bound.
No kernel may reach another device: no remote copies, remote signals or barrier semaphores. Data moves between devices by JAX's collectives and lax.ppermute only.
A program may use at most 128 MiB of HBM per device.

v0:
```python
import functools
import math

import jax
import jax.numpy as jnp
from jax import lax
from jax.experimental import pallas as pl
from jax.experimental.pallas import tpu as pltpu
from jax.sharding import PartitionSpec as P

ALL = ("gx", "gy")
HEAD_DIM = 64
HALO = 128
BLK = 256
D = 1280
HALF = D // 2
PAIR = 2 * HEAD_DIM
STEPS = D // (2 * PAIR)
PIECES = 3
WIDTHS = (HALF, 512)
GATHERED = sum(WIDTHS)
SCALE_LOG2 = 0.125 * math.log2(math.e)


def flat_pairs(move):
    pairs = []
    for gx in range(8):
        for gy in range(32):
            x, y_lo, z, y_hi, core = move(gx // 2, gx % 2, gy // 4, (gy // 2) % 2, gy % 2)
            pairs.append((gx * 32 + gy, (x % 4 * 2 + y_lo) * 32 + z % 8 * 4 + y_hi * 2 + core))
    return pairs


CORE_SWAP = flat_pairs(lambda x, l, z, h, c: (x, l, z, h, 1 - c))
CROSS_SWAP = flat_pairs(lambda x, l, z, h, c: (x, 1 - l, z, 1 - h, c))
FAR_SWAP = flat_pairs(lambda x, l, z, h, c: (x, 1 - l, z, 1 - h, 1 - c))
X_UP = flat_pairs(lambda x, l, z, h, c: (x + 1, l, z, h, c))
X_DOWN = flat_pairs(lambda x, l, z, h, c: (x - 1, l, z, h, c))
Z_GROUPS = [[z * 4 + k for z in range(8)] for k in range(4)]


def lookup(table, index):
    return jnp.sum(jnp.where(jnp.arange(table.shape[0], dtype=jnp.int32) == index, table, 0))


def lookup_all(table, index):
    ids = jnp.arange(table.shape[0], dtype=jnp.int32)
    return jnp.sum(jnp.where(ids[None, :] == index[:, None], table[None, :], 0), axis=1)


def standardized(rows):
    values = rows.astype(jnp.float32)
    mean = jnp.mean(values, axis=-1, keepdims=True)
    centred = values - mean
    variance = jnp.mean(centred * centred, axis=-1, keepdims=True)
    return (centred * lax.rsqrt(variance + 1e-05)).astype(jnp.bfloat16)


def layer_kernel(first_block, with_out, scal, lengths, matchings, *refs):
    width_here = WIDTHS[0 if with_out else 1]
    tiles = width_here // PAIR
    own_at = 0 if with_out else WIDTHS[0]
    sources, refs = (refs[:PIECES], refs[PIECES : 2 * PIECES]), refs[2 * PIECES :]
    if first_block:
        own, refs = refs[0], refs[1:]
    if with_out:
        collected, out, normed, ctx, weights, weight_sems, out_weights, out_sems, spare = refs
    else:
        other, tail, out, normed, ctx, weights, weight_sems = refs
    step = pl.program_id(0)
    here, core, x = scal[0], scal[1], scal[2]
    block = here if first_block else matchings[1, here]
    partner = matchings[0 if with_out else 1, block]
    known = jnp.minimum(lengths[jnp.maximum(block - 1, 0)], HALO)
    known = jnp.where(block > 0, known, 0)

    def slot_half(at, half):
        rows = pl.ds(half * 1024 + at, HALO, stride=8)
        return jnp.concatenate([spare[i, rows, :] for i in range(HALF // 128)], axis=1)

    def start_tile(half, x_here, index, target, width, sem):
        place = (index // tiles - x_here) % 4
        column = index % tiles * PAIR
        if place % 2 == 0:
            piece = 0
            column += own_at + place // 2 * GATHERED
        else:
            piece = 1 + place // 2
        source = sources[half][piece].at[:, pl.ds(column, width)]
        pltpu.make_async_copy(source, target, sem).start()

    @pl.when(step == 0)
    def _():
        for x_here in range(4):

            @pl.when(x == x_here)
            def _():
                for at in range(STEPS):
                    for kind in range(3):
                        for half in range(2):
                            start_tile(
                                half,
                                x_here,
                                kind * STEPS + at,
                                weights.at[at, kind, :, pl.ds(half * PAIR, PAIR)],
                                PAIR,
                                weight_sems.at[at, kind, half],
                            )
                if with_out:
                    for half in range(2):
                        start_tile(
                            half, x_here, 3 * STEPS, out_weights.at[half], HALF, out_sems.at[half]
                        )

        if with_out:
            for lane_tile in range(HALF // 128):
                lanes = pl.ds(lane_tile * 128, 128)
                spare[lane_tile] = collected[:, lanes].astype(jnp.float32)

            def slot(at):
                return jnp.concatenate([slot_half(at, 0), slot_half(at, 1)], axis=1)

            slots = (0, 1, 7) if first_block else (2, 3, 4, 5, 6)
            if first_block:
                normed[pl.ds(0, BLK), :] = standardized(own[...])
            base = BLK if first_block else 0
            for order, at in enumerate(slots):
                normed[pl.ds(base + order * HALO, HALO), :] = standardized(slot(at))
        else:
            normed[pl.ds(0, BLK), :] = standardized(own[...])
            normed[pl.ds(BLK, BLK), :] = standardized(other[...])
            normed[pl.ds(2 * BLK, HALO), :] = standardized(tail[...])

    for kind in range(3):
        for half in range(2):
            target = weights.at[step, kind, :, pl.ds(half * PAIR, PAIR)]
            pltpu.make_async_copy(target, target, weight_sems.at[step, kind, half]).wait()

    count = 2 * BLK + HALO
    row = lax.broadcasted_iota(jnp.int32, (count, PAIR), 0)
    lane_k = lax.broadcasted_iota(jnp.int32, (count, PAIR), 1)
    lane_q = lax.broadcasted_iota(jnp.int32, (BLK, PAIR), 1)
    limit = jnp.where(
        row < BLK,
        lengths[block],
        jnp.where(row < 2 * BLK, lengths[partner] + BLK, known + 2 * BLK),
    )
    bias = jnp.where(row < limit, 0.0, -1e30).astype(jnp.float32)

    x_all = normed[...]
    dot = functools.partial(jnp.dot, preferred_element_type=jnp.float32)
    q = dot(normed[pl.ds(0, BLK), :], weights[step, 0])
    k = dot(x_all, weights[step, 1])
    v = dot(x_all, weights[step, 2]).astype(jnp.bfloat16)
    for pair in range(2):
        lanes = slice(pair * PAIR, (pair + 1) * PAIR)
        q_pair, k_pair, v_pair = q[:, lanes], k[:, lanes], v[:, lanes]
        parts = []
        for head in range(2):
            mine_q = (lane_q < HEAD_DIM) if head == 0 else (lane_q >= HEAD_DIM)
            free = HEAD_DIM if head == 0 else 0
            q_head = jnp.where(
                mine_q, q_pair, jnp.where(lane_q == free, 1.0, 0.0)
            ).astype(jnp.bfloat16)
            k_head = jnp.where(lane_k == free, bias, k_pair).astype(jnp.bfloat16)
            scores = lax.dot_general(
                q_head, k_head, (((1,), (1,)), ((), ())), preferred_element_type=jnp.float32
            )
            top = jnp.max(scores, axis=-1, keepdims=True)
            expo = jnp.exp2((scores - top) * SCALE_LOG2)
            total = jnp.sum(expo, axis=-1, keepdims=True)
            mixed = dot(expo.astype(jnp.bfloat16), v_pair)
            parts.append(mixed / total)
        both = jnp.where(lane_q < HEAD_DIM, parts[0], parts[1]).astype(jnp.bfloat16)
        half = core if pair == 0 else 1 - core
        place = pl.multiple_of((half * STEPS + step) * PAIR, PAIR)
        ctx[:, pl.ds(place, PAIR)] = both

    @pl.when(step == STEPS - 1)
    def _():
        if with_out:
            context = ctx[...]
            for half in range(2):
                target = out_weights.at[half]
                pltpu.make_async_copy(target, target, out_sems.at[half]).wait()
                update = dot(context, target[...])
                absolute = core if half == 0 else 1 - core
                if first_block:
                    place = pl.ds(pl.multiple_of(absolute * HALF, 128), HALF)
                    here_rows = own[:, place].astype(jnp.float32)
                    out[:, place] = (here_rows + update).astype(jnp.bfloat16)
                else:
                    place = pl.ds(pl.multiple_of(absolute * HALF, 128), HALF)
                    for part in range(2):
                        rows = pl.ds(part * HALO, HALO)
                        change = update[part * HALO : (part + 1) * HALO]
                        out[rows, place] = (slot_half(2 + part, absolute) + change).astype(
                            jnp.bfloat16
                        )
        else:
            out[...] = ctx[...]


def layer(scal, lengths, matchings, mine, yours, rows, first_block, with_out):
    hbm = pl.BlockSpec(memory_space=pl.ANY)
    whole = [pl.BlockSpec(r.shape, lambda i, *s: (0, 0)) for r in rows]
    scratch = [
        pltpu.VMEM((2 * BLK + HALO, D), jnp.bfloat16),
        pltpu.VMEM((BLK, D), jnp.bfloat16),
        pltpu.VMEM((STEPS, 3, D, 2 * PAIR), jnp.bfloat16),
        pltpu.SemaphoreType.DMA((STEPS, 3, 2)),
    ]
    if with_out:
        scratch += [
            pltpu.VMEM((2, D, HALF), jnp.bfloat16),
            pltpu.SemaphoreType.DMA((2,)),
            pltpu.VMEM((HALF // 128, 2048, 128), jnp.float32),
        ]
    return pl.pallas_call(
        functools.partial(layer_kernel, first_block, with_out),
        grid_spec=pltpu.PrefetchScalarGridSpec(
            num_scalar_prefetch=3,
            grid=(STEPS,),
            in_specs=[hbm] * (2 * PIECES) + whole,
            out_specs=pl.BlockSpec((BLK, D), lambda i, *s: (0, 0)),
            scratch_shapes=scratch,
        ),
        out_shape=jax.ShapeDtypeStruct((BLK, D), jnp.bfloat16),
        compiler_params=pltpu.CompilerParams(
            dimension_semantics=("arbitrary",), vmem_limit_bytes=60 * 1024 * 1024
        ),
        cost_estimate=pl.CostEstimate(
            flops=8 * 10**9, bytes_accessed=14 * 10**6, transcendentals=4 * 10**6
        ),
    )(scal, lengths, matchings, *mine, *yours, *rows)


def next_to(block):
    return lax.ppermute(block, ALL, X_DOWN), lax.ppermute(block, ALL, X_UP)


def other_core(pieces):
    return tuple(lax.ppermute(piece, ALL, CORE_SWAP) for piece in pieces)


def gather_rows(wqkv, wout, x, core, y_hi):
    first = jnp.concatenate([wqkv[0], wout[0]], axis=1)
    second = wqkv[1].reshape(-1, 3, 2, HALF)

    def column_block(half):
        part_1 = lax.dynamic_index_in_dim(second, half, 2, keepdims=False).reshape(-1, 3 * HALF)
        part_1 = jnp.pad(part_1, ((0, 0), (0, 128)))
        parts = []
        for place in (x, (x + 2) & 3):
            parts.append(lax.dynamic_slice_in_dim(first, (place * 2 + half) * HALF, HALF, 1))
            parts.append(lax.dynamic_slice_in_dim(part_1, place * WIDTHS[1], WIDTHS[1], 1))
        return jnp.concatenate(parts, axis=1)

    keep, give = column_block(core), column_block(1 - core)
    near = lax.ppermute(give, ALL, CORE_SWAP)
    cross = lax.ppermute(keep, ALL, CROSS_SWAP)
    far = lax.ppermute(give, ALL, FAR_SWAP)

    def in_order(mine_first, mine, yours):
        return jnp.where(
            mine_first,
            jnp.concatenate([mine, yours], axis=0),
            jnp.concatenate([yours, mine], axis=0),
        )

    return in_order(
        y_hi == 0, in_order(core == 0, keep, near), in_order(core == 0, cross, far)
    )


def local(frames, lengths, matchings, wqkv, wout):
    gx, gy = lax.axis_index("gx"), lax.axis_index("gy")
    here = gx * 32 + gy
    core, y_hi, x = gy & 1, (gy >> 1) & 1, gx >> 1
    plane = gather_rows(wqkv, wout, x, core, y_hi)

    spread_in = frames.reshape(2, HALO, 2, HALF).transpose(2, 1, 0, 3).reshape(256, 2, HALF)
    plane, spread_in = lax.optimization_barrier((plane, spread_in))
    columns = lax.all_gather(plane, "gy", axis=0, tiled=True, axis_index_groups=Z_GROUPS)
    spread = lax.all_to_all(spread_in, ALL, 0, 0, tiled=True).reshape(512, HALF)

    partner_0, partner_1 = matchings[0], matchings[1]
    second = lookup_all(partner_0, partner_1)
    before = jnp.maximum(jnp.arange(256, dtype=jnp.int32) - 1, 0)
    before_1 = jnp.maximum(partner_1 - 1, 0)
    high = ((here & (HALO - 1)) < jnp.maximum(lengths - HALO, 0)).astype(jnp.int32)
    wanted = jnp.stack(
        [
            2 * partner_0,
            2 * partner_0 + 1,
            2 * partner_1,
            2 * partner_1 + 1,
            2 * second,
            2 * second + 1,
            2 * before_1 + lookup_all(high, before_1),
            2 * before + lookup_all(high, before),
        ],
        axis=1,
    ).reshape(-1)
    chosen = (wanted[:, None] == jnp.arange(512, dtype=jnp.int32)[None, :]).astype(jnp.bfloat16)
    routed = jnp.dot(chosen, spread, preferred_element_type=jnp.float32).astype(jnp.bfloat16)
    columns, _ = lax.optimization_barrier((columns, routed))
    collected = lax.all_to_all(routed.reshape(256, 8, HALF), ALL, 0, 0, tiled=True)
    collected = collected.reshape(2048, HALF)

    yours = lax.ppermute(columns, ALL, CORE_SWAP)
    near_0 = next_to(columns[:, : WIDTHS[0]])
    mine_0, yours_0 = (columns, *near_0), (yours, *other_core(near_0))
    block_1, near_0 = lax.optimization_barrier((columns[:, WIDTHS[0] : GATHERED], near_0))
    near_1 = next_to(block_1)

    scal = jnp.stack([here, core, x]).astype(jnp.int32)
    run = functools.partial(layer, scal, lengths, matchings)
    hidden = run(mine_0, yours_0, (frames, collected), True, True)
    tail_start = jnp.maximum(lookup(lengths, here) - HALO, 0)
    own_tail = lax.dynamic_slice_in_dim(hidden, tail_start, HALO, 0)
    tail = lax.ppermute(own_tail, ALL, [(i, i + 1) for i in range(255)])
    near_1, hidden = lax.optimization_barrier((near_1, hidden))
    mine_1, yours_1 = (columns, *near_1), (yours, *other_core(near_1))
    hidden_1 = run(mine_0, yours_0, (collected,), False, True)
    context = run(mine_1, yours_1, (hidden, hidden_1, tail), True, False)
    return hidden, context


def solution(mesh):
    rows = P(ALL, None)
    return jax.shard_map(
        local,
        mesh=mesh,
        in_specs=(rows, P(), P(), P(None, "gy", None), P(None, "gy", None)),
        out_specs=(rows, rows),
        check_vma=False,
    )
```

profile of v0, /device:TPU:1, one launch (start us, length us, event | category | flops | bytes accessed | tf_op | source)
XLA Modules:
  0.0 281.1 jit_solution(3433720681600254575)
XLA Ops:
  7.2 0.0 all-gather.2.cloned.1.call-start
  7.2 1.1 slice_bitcast_fusion
  8.4 0.1 reshape_squeeze.3
  8.5 0.0 copy-start.1
  8.5 2.0 dynamic-slice_reduce_fusion.1
  10.5 0.2 fusion.4
  10.7 3.3 %collective-permute-start = (bf16[40,2304]{1,0:T(8,128)(2,1)S(1)}, bf16[40,2304]{1,0:T(8,128)(2,1)S(1)}, u32[]{:S(2)}, u32[]{:S(2)}) collective-permute-start(bf16[40,2304]{1,0:T(8,128)(2,1)S(1)} %pad_maximum_fusion.1), channel_id=1, source_target_pairs={{0,1},{1,0},{2,3},{3,2},{4,5},{5,4},{6,7},{7,6},{8,9},{9,8},{10,11... | collective-permute-start | bytes 552968 | tf_op jit(solution)/shard_map/ppermute | solution.py:260
  14.1 1.0 collective-permute-start.2
  15.1 1.8 collective-permute-start.1
  16.9 0.1 reshape.140
  17.1 0.1 copy.24
  17.1 0.0 collective-permute-done
  17.1 0.1 maximum_select_fusion.1
  17.2 0.0 copy-start.3
  17.2 0.0 copy-start.4
  17.2 8.1 %collective-permute-done.1 = bf16[40,2304]{1,0:T(8,128)(2,1)S(1)} collective-permute-done((bf16[40,2304]{1,0:T(8,128)(2,1)S(1)}, bf16[40,2304]{1,0:T(8,128)(2,1)S(1)}, u32[]{:S(2)}, u32[]{:S(2)}) %collective-permute-start.1) | collective-permute-done | bytes 184352 | tf_op jit(solution)/shard_map/ppermute | solution.py:261
  25.3 0.0 collective-permute-done.2
  25.3 0.1 maximum_select_fusion.2
  25.4 1.0 maximum_select_fusion
  26.4 0.0 all-gather.2.cloned.1.call-update
  26.5 0.6 fusion.7
  27.1 1.5 copy.26
  28.6 13.2 %all-to-all-start = ((bf16[256,2,640]{2,1,0:T(2,128)(2,1)}), bf16[256,2,640]{2,1,0:T(2,128)(2,1)S(1)}, u32[]{:S(2)}, u32[]{:S(2)}) async-start(bf16[256,2,640]{2,1,0:T(2,128)(2,1)} %copy.26), calls=%async_computation | async-start | bytes 1310720 | tf_op jit(solution)/shard_map/all_to_all | solution.py:285
  41.8 0.2 select_reduce_fusion.2
  42.0 0.2 select_reduce_fusion
  42.3 0.1 copy.25
  42.4 0.1 eq.81
  42.6 30.2 %all-to-all-done = bf16[256,2,640]{2,1,0:T(2,128)(2,1)S(1)} async-done(((bf16[256,2,640]{2,1,0:T(2,128)(2,1)}), bf16[256,2,640]{2,1,0:T(2,128)(2,1)S(1)}, u32[]{:S(2)}, u32[]{:S(2)}) %all-to-all-start) | async-done | bytes 655392 | tf_op jit(solution)/shard_map/all_to_all | solution.py:285
  72.7 0.2 reshape.142
  73.0 3.3 %fusion.1 = bf16[2048,640]{1,0:T(8,128)(2,1)} fusion(bf16[512,640]{1,0:T(8,128)(2,1)S(1)} %reshape.142, s32[2048]{0:T(1024)S(1)} %eq.81), kind=kOutput, calls=%fused_computation.2 | convolution fusion | flops 1344536576 | bytes 3284992 | tf_op jit(solution)/shard_map/dot_general | solution.py:306
  76.2 36.5 %all-gather.2.cloned.1.call-done.refs_0_ = bf16[1280,2304]{1,0:T(8,128)(2,1)} async-done(((bf16[160,2304]{1,0:T(8,128)(2,1)}), bf16[1280,2304]{1,0:T(8,128)(2,1)}) %all-gather.2.cloned.1.call-update) | async-done | bytes 5898256 | tf_op jit(solution)/shard_map/all_gather | solution.py:284
  112.7 0.7 collective-permute-start.7
  113.4 9.9 %all-to-all-start.1 = ((bf16[256,8,640]{2,1,0:T(8,128)(2,1)}), bf16[256,8,640]{2,1,0:T(8,128)(2,1)S(1)}, u32[]{:S(2)}, u32[]{:S(2)}) async-start(bf16[256,8,640]{2,1,0:T(8,128)(2,1)} %bitcast.32), calls=%async_computation.1 | async-start | bytes 5242880 | tf_op jit(solution)/shard_map/all_to_all | solution.py:308
  123.3 1.6 slice.23
  124.9 2.7 collective-permute-start.3
  127.6 0.0 collective-permute-start.4
  127.6 59.5 %collective-permute-done.3.refs_1_ = bf16[1280,640]{1,0:T(8,128)(2,1)} collective-permute-done((bf16[1280,640]{1,0:T(8,128)(2,1)S(1)}, bf16[1280,640]{1,0:T(8,128)(2,1)}, u32[]{:S(2)}, u32[]{:S(2)}) %collective-permute-start.3) | collective-permute-done | bytes 1638432 | tf_op jit(solution)/shard_map/ppermute | solution.py:239
  187.1 1.0 collective-permute-start.8
  188.1 1.0 collective-permute-done.4.refs_2_
  189.2 1.1 collective-permute-start.9
  190.3 2.5 slice.22
  192.7 0.4 collective-permute-start.5
  193.1 1.1 collective-permute-start.6
  194.2 0.7 pad_add_fusion.scal
  194.9 0.0 all-to-all-done.1
  194.9 0.0 collective-permute-done.8.refs_4_
  194.9 0.0 collective-permute-done.9.refs_5_
  194.9 0.0 collective-permute-done.7.refs_3_
  194.9 1.5 copy-done
  196.4 20.6 %shard_map.68.refs_6_ = bf16[256,1280]{1,0:T(8,128)(2,1)} custom-call(s32[3]{0:T(128)} %pad_add_fusion.scal, s32[256]{0:T(256)} %lengths.5, s32[2,256]{1,0:T(2,128)} %matchings.5, bf16[1280,2304]{1,0:T(8,128)(2,1)} %all-gather.2.cloned.1.call-done.refs_0_, bf16[1280,640]{1,0:T(8,128)(2,1)} %collective-permute-done.3.refs_1_, ...), custom_call_target="tpu_custom_call" | custom-call | flops 8000000000 | bytes 14000000 | tf_op jit(solution)/shard_map/pallas_call | solution.py:219
  217.0 6.5 %collective-permute-done.5.refs_1_ = bf16[1280,512]{1,0:T(8,128)(2,1)} collective-permute-done((bf16[1280,512]{1,0:T(8,128)(2,1)}, bf16[1280,512]{1,0:T(8,128)(2,1)}, u32[]{:S(2)}, u32[]{:S(2)}) %collective-permute-start.5) | collective-permute-done | bytes 1310752 | tf_op jit(solution)/shard_map/ppermute | solution.py:239
  223.5 0.7 collective-permute-done.6.refs_2_
  224.1 1.7 collective-permute-start.10
  225.8 0.0 collective-permute-start.11
  226.4 1.1 constant_dynamic-slice_fusion
  227.4 5.1 %collective-permute-start.12 = (bf16[128,1280]{1,0:T(8,128)(2,1)S(1)}, bf16[128,1280]{1,0:T(8,128)(2,1)S(1)}, u32[]{:S(2)}, u32[]{:S(2)}) collective-permute-start(bf16[128,1280]{1,0:T(8,128)(2,1)S(1)} %constant_dynamic-slice_fusion), channel_id=1, source_target_pairs={{0,1},{1,2},{2,3},{3,4},{4,5},{5,6},{6,7},{7,8},{8,9},{9,10},{10,1... | collective-permute-start | bytes 983048 | tf_op jit(solution)/shard_map/ppermute | solution.py:322
  232.5 20.7 %shard_map.69.refs_7_ = bf16[256,1280]{1,0:T(8,128)(2,1)} custom-call(s32[3]{0:T(128)} %pad_add_fusion.scal, s32[256]{0:T(256)} %lengths.5, s32[2,256]{1,0:T(2,128)} %matchings.5, bf16[1280,2304]{1,0:T(8,128)(2,1)} %all-gather.2.cloned.1.call-done.refs_0_, bf16[1280,640]{1,0:T(8,128)(2,1)} %collective-permute-done.3.refs_1_, ...), custom_call_target="tpu_custom_call" | custom-call | flops 8000000000 | bytes 14000000 | tf_op jit(solution)/shard_map/pallas_call | solution.py:219
  253.3 0.0 collective-permute-done.12.refs_8_
  253.3 0.0 collective-permute-done.10.refs_4_
  253.3 0.0 collective-permute-done.11.refs_5_
  253.3 0.7 copy-done.7
  254.1 0.5 copy-done.5
  254.6 1.1 copy-done.6
  255.6 18.6 %shard_map.70 = bf16[256,1280]{1,0:T(8,128)(2,1)} custom-call(s32[3]{0:T(128)} %pad_add_fusion.scal, s32[256]{0:T(256)} %lengths.5, s32[2,256]{1,0:T(2,128)} %matchings.5, bf16[1280,2304]{1,0:T(8,128)(2,1)} %all-gather.2.cloned.1.call-done.refs_0_, bf16[1280,512]{1,0:T(8,128)(2,1)} %collective-permute-done.5.refs_1_, ...), custom_call_target="tpu_custom_call" | custom-call | flops 8000000000 | bytes 14000000 | tf_op jit(solution)/shard_map/pallas_call | solution.py:219
  (23 shorter events, 0.2 us)
Async XLA Ops:
  7.2 105.6 %all-gather.2.cloned.1.call-start = ((), (), s32[]{:S(2)}) async-start(), calls=%async_computation.2 | async-start | bytes 6635520 | tf_op jit(solution)/shard_map/all_gather | solution.py:284
  7.2 3.3 %copy-start.2 = (bf16[1,40,1280]{2,1,0:T(8,128)(2,1)S(1)}, bf16[1,40,1280]{2,1,0:T(8,128)(2,1)}, u32[]{:S(2)}) copy-start(bf16[1,40,1280]{2,1,0:T(8,128)(2,1)} %param.9) | copy-start | bytes 307204
  8.5 8.4 %copy-start.1 = (bf16[256,1280]{1,0:T(8,128)(2,1)S(1)}, bf16[256,1280]{1,0:T(8,128)(2,1)}, u32[]{:S(2)}) copy-start(bf16[256,1280]{1,0:T(8,128)(2,1)} %refs_6_.1) | copy-start | bytes 1966084
  10.7 6.4 %collective-permute-start = (bf16[40,2304]{1,0:T(8,128)(2,1)S(1)}, bf16[40,2304]{1,0:T(8,128)(2,1)S(1)}, u32[]{:S(2)}, u32[]{:S(2)}) collective-permute-start(bf16[40,2304]{1,0:T(8,128)(2,1)S(1)} %pad_maximum_fusion.1), channel_id=1, source_target_pairs={{0,1},{1,0},{2,3},{3,2},{4,5},{5,4},{6,7},{7,6},{8,9},{9,8},{10,11... | collective-permute-start | bytes 552968 | tf_op jit(solution)/shard_map/ppermute | solution.py:260
  14.1 11.3 %collective-permute-start.2 = (bf16[40,2304]{1,0:T(8,128)(2,1)S(1)}, bf16[40,2304]{1,0:T(8,128)(2,1)S(1)}, u32[]{:S(2)}, u32[]{:S(2)}) collective-permute-start(bf16[40,2304]{1,0:T(8,128)(2,1)S(1)} %pad_maximum_fusion.1), channel_id=1, source_target_pairs={{0,35},{1,34},{2,33},{3,32},{4,39},{5,38},{6,37},{7,36},{8,43},{9,... | collective-permute-start | bytes 552968 | tf_op jit(solution)/shard_map/ppermute | solution.py:262
  15.1 10.2 %collective-permute-start.1 = (bf16[40,2304]{1,0:T(8,128)(2,1)S(1)}, bf16[40,2304]{1,0:T(8,128)(2,1)S(1)}, u32[]{:S(2)}, u32[]{:S(2)}) collective-permute-start(bf16[40,2304]{1,0:T(8,128)(2,1)S(1)} %pad_maximum_fusion), channel_id=1, source_target_pairs={{0,34},{1,35},{2,32},{3,33},{4,38},{5,39},{6,36},{7,37},{8,42},{9,... | collective-permute-start | bytes 552968 | tf_op jit(solution)/shard_map/ppermute | solution.py:261
  17.2 9.2 %copy-start.3 = (s32[2,256]{1,0:T(2,128)S(1)}, s32[2,256]{1,0:T(2,128)}, u32[]{:S(2)}) copy-start(s32[2,256]{1,0:T(2,128)} %matchings.5) | copy-start | bytes 6148
  17.2 9.2 %copy-start.4 = (s32[256]{0:T(256)S(1)}, s32[256]{0:T(256)}, u32[]{:S(2)}) copy-start(s32[256]{0:T(256)} %lengths.5) | copy-start | bytes 3076
  28.6 44.1 %all-to-all-start = ((bf16[256,2,640]{2,1,0:T(2,128)(2,1)}), bf16[256,2,640]{2,1,0:T(2,128)(2,1)S(1)}, u32[]{:S(2)}, u32[]{:S(2)}) async-start(bf16[256,2,640]{2,1,0:T(2,128)(2,1)} %copy.26), calls=%async_computation | async-start | bytes 1310720 | tf_op jit(solution)/shard_map/all_to_all | solution.py:285
  112.7 82.1 %collective-permute-start.7 = (bf16[1280,2304]{1,0:T(8,128)(2,1)}, bf16[1280,2304]{1,0:T(8,128)(2,1)}, u32[]{:S(2)}, u32[]{:S(2)}) collective-permute-start(bf16[1280,2304]{1,0:T(8,128)(2,1)} %all-gather.2.cloned.1.call-done.refs_0_), channel_id=1, source_target_pairs={{0,1},{1,0},{2,3},{3,2},{4,5},{5,4},{6,7},{7,6},{8,9},{9,8},{10,11... | collective-permute-start | bytes 17694728 | tf_op jit(solution)/shard_map/ppermute | solution.py:311
  113.4 81.4 %all-to-all-start.1 = ((bf16[256,8,640]{2,1,0:T(8,128)(2,1)}), bf16[256,8,640]{2,1,0:T(8,128)(2,1)S(1)}, u32[]{:S(2)}, u32[]{:S(2)}) async-start(bf16[256,8,640]{2,1,0:T(8,128)(2,1)} %bitcast.32), calls=%async_computation.1 | async-start | bytes 5242880 | tf_op jit(solution)/shard_map/all_to_all | solution.py:308
  124.9 62.2 %collective-permute-start.3 = (bf16[1280,640]{1,0:T(8,128)(2,1)S(1)}, bf16[1280,640]{1,0:T(8,128)(2,1)}, u32[]{:S(2)}, u32[]{:S(2)}) collective-permute-start(bf16[1280,640]{1,0:T(8,128)(2,1)S(1)} %slice.23), channel_id=1, source_target_pairs={{0,192},{1,193},{2,194},{3,195},{4,196},{5,197},{6,198},{7,199},{8... | collective-permute-start | bytes 4915208 | tf_op jit(solution)/shard_map/ppermute | solution.py:239
  127.6 61.6 %collective-permute-start.4 = (bf16[1280,640]{1,0:T(8,128)(2,1)S(1)}, bf16[1280,640]{1,0:T(8,128)(2,1)}, u32[]{:S(2)}, u32[]{:S(2)}) collective-permute-start(bf16[1280,640]{1,0:T(8,128)(2,1)S(1)} %slice.23), channel_id=1, source_target_pairs={{0,64},{1,65},{2,66},{3,67},{4,68},{5,69},{6,70},{7,71},{8,72},{9,... | collective-permute-start | bytes 4915208 | tf_op jit(solution)/shard_map/ppermute | solution.py:239
  187.1 7.8 %collective-permute-start.8 = (bf16[1280,640]{1,0:T(8,128)(2,1)}, bf16[1280,640]{1,0:T(8,128)(2,1)}, u32[]{:S(2)}, u32[]{:S(2)}) collective-permute-start(bf16[1280,640]{1,0:T(8,128)(2,1)} %collective-permute-done.3.refs_1_), channel_id=1, source_target_pairs={{0,1},{1,0},{2,3},{3,2},{4,5},{5,4},{6,7},{7,6},{8,9},{9,8},{10,11... | collective-permute-start | bytes 4915208 | tf_op jit(solution)/shard_map/ppermute | solution.py:243
  189.2 5.7 %collective-permute-start.9 = (bf16[1280,640]{1,0:T(8,128)(2,1)}, bf16[1280,640]{1,0:T(8,128)(2,1)}, u32[]{:S(2)}, u32[]{:S(2)}) collective-permute-start(bf16[1280,640]{1,0:T(8,128)(2,1)} %collective-permute-done.4.refs_2_), channel_id=1, source_target_pairs={{0,1},{1,0},{2,3},{3,2},{4,5},{5,4},{6,7},{7,6},{8,9},{9,8},{10,11... | collective-permute-start | bytes 4915208 | tf_op jit(solution)/shard_map/ppermute | solution.py:243
  192.7 30.7 %collective-permute-start.5 = (bf16[1280,512]{1,0:T(8,128)(2,1)}, bf16[1280,512]{1,0:T(8,128)(2,1)}, u32[]{:S(2)}, u32[]{:S(2)}) collective-permute-start(bf16[1280,512]{1,0:T(8,128)(2,1)} %slice.22), channel_id=1, source_target_pairs={{0,192},{1,193},{2,194},{3,195},{4,196},{5,197},{6,198},{7,199},{8... | collective-permute-start | bytes 3932168 | tf_op jit(solution)/shard_map/ppermute | solution.py:239
  193.1 31.0 %collective-permute-start.6 = (bf16[1280,512]{1,0:T(8,128)(2,1)}, bf16[1280,512]{1,0:T(8,128)(2,1)}, u32[]{:S(2)}, u32[]{:S(2)}) collective-permute-start(bf16[1280,512]{1,0:T(8,128)(2,1)} %slice.22), channel_id=1, source_target_pairs={{0,64},{1,65},{2,66},{3,67},{4,68},{5,69},{6,70},{7,71},{8,72},{9,... | collective-permute-start | bytes 3932168 | tf_op jit(solution)/shard_map/ppermute | solution.py:239
  194.9 1.5 copy-start
  224.1 29.2 %collective-permute-start.10 = (bf16[1280,512]{1,0:T(8,128)(2,1)}, bf16[1280,512]{1,0:T(8,128)(2,1)S(1)}, u32[]{:S(2)}, u32[]{:S(2)}) collective-permute-start(bf16[1280,512]{1,0:T(8,128)(2,1)} %collective-permute-done.5.refs_1_), channel_id=1, source_target_pairs={{0,1},{1,0},{2,3},{3,2},{4,5},{5,4},{6,7},{7,6},{8,9},{9,8},{10,11... | collective-permute-start | bytes 3932168 | tf_op jit(solution)/shard_map/ppermute | solution.py:243
  225.8 27.5 %collective-permute-start.11 = (bf16[1280,512]{1,0:T(8,128)(2,1)}, bf16[1280,512]{1,0:T(8,128)(2,1)S(1)}, u32[]{:S(2)}, u32[]{:S(2)}) collective-permute-start(bf16[1280,512]{1,0:T(8,128)(2,1)} %collective-permute-done.6.refs_2_), channel_id=1, source_target_pairs={{0,1},{1,0},{2,3},{3,2},{4,5},{5,4},{6,7},{7,6},{8,9},{9,8},{10,11... | collective-permute-start | bytes 3932168 | tf_op jit(solution)/shard_map/ppermute | solution.py:243
  227.4 25.8 %collective-permute-start.12 = (bf16[128,1280]{1,0:T(8,128)(2,1)S(1)}, bf16[128,1280]{1,0:T(8,128)(2,1)S(1)}, u32[]{:S(2)}, u32[]{:S(2)}) collective-permute-start(bf16[128,1280]{1,0:T(8,128)(2,1)S(1)} %constant_dynamic-slice_fusion), channel_id=1, source_target_pairs={{0,1},{1,2},{2,3},{3,4},{4,5},{5,6},{6,7},{7,8},{8,9},{9,10},{10,1... | collective-permute-start | bytes 983048 | tf_op jit(solution)/shard_map/ppermute | solution.py:322
  253.3 0.8 copy-start.7
  253.3 1.2 copy-start.5
  254.6 1.1 copy-start.6
Sparse Core Ops, SparseCore 0:
  26.5 86.1 all-gather.1
where the time goes:
time: 282 us; the launch traced here: 281 us
  waiting for transfers between devices  142 us (50%)
  Pallas kernels  59.9 us (21%)
  starting transfers between devices  42.9 us (15%)
  between operations  15 us (5%)
  local copies, waits for them, and re-layouts  14.4 us (5%)
  matrix products  3.27 us (1%)
  other arithmetic  3.08 us (1%)
    ppermute x4, waiting for transfers between devices, next_to(): return (lax.ppermute(block, ALL, X_DOWN), lax.ppermute(block, ALL, X_UP))  67.7 us
    pallas_call x3, Pallas kernels, layer(): pl.pallas_call(functools.partial(layer_kernel, first_block, with_out), gr...  59.9 us
    all_gather x1, waiting for transfers between devices, local(): lax.all_gather(plane, 'gy', axis=0, tiled=True, axis_index_groups=Z_GROUPS)  36.5 us
    all_to_all x1, waiting for transfers between devices, local(): spread = lax.all_to_all(spread_in, ALL, 0, 0, tiled=True).reshape(512, HALF)  30.2 us
    all_to_all x1, starting transfers between devices, local(): spread = lax.all_to_all(spread_in, ALL, 0, 0, tiled=True).reshape(512, HALF)  13.2 us
    all_to_all x1, starting transfers between devices, local(): lax.all_to_all(routed.reshape(256, 8, HALF), ALL, 0, 0, tiled=True)  9.9 us
    ppermute x1, waiting for transfers between devices, gather_rows(): cross = lax.ppermute(keep, ALL, CROSS_SWAP)  8.08 us
  transfers between devices with their start and end apart: 16, of which 7 were waited for; matrix products, arithmetic and copies ran while one was open for 4% of the time, Pallas kernels for 15%

commit v1 on v0

--- a/solution.py
+++ b/solution.py
@@ -18,7 +18,6 @@
 STEPS = D // (2 * PAIR)
 PIECES = 3
 WIDTHS = (HALF, 512)
-GATHERED = sum(WIDTHS)
 SCALE_LOG2 = 0.125 * math.log2(math.e)
 
 
@@ -59,7 +58,6 @@
 def layer_kernel(first_block, with_out, scal, lengths, matchings, *refs):
     width_here = WIDTHS[0 if with_out else 1]
     tiles = width_here // PAIR
-    own_at = 0 if with_out else WIDTHS[0]
     sources, refs = (refs[:PIECES], refs[PIECES : 2 * PIECES]), refs[2 * PIECES :]
     if first_block:
         own, refs = refs[0], refs[1:]
@@ -83,7 +81,7 @@
         column = index % tiles * PAIR
         if place % 2 == 0:
             piece = 0
-            column += own_at + place // 2 * GATHERED
+            column += place // 2 * width_here
         else:
             piece = 1 + place // 2
         source = sources[half][piece].at[:, pl.ds(column, width)]
@@ -250,11 +248,10 @@
     def column_block(half):
         part_1 = lax.dynamic_index_in_dim(second, half, 2, keepdims=False).reshape(-1, 3 * HALF)
         part_1 = jnp.pad(part_1, ((0, 0), (0, 128)))
-        parts = []
-        for place in (x, (x + 2) & 3):
-            parts.append(lax.dynamic_slice_in_dim(first, (place * 2 + half) * HALF, HALF, 1))
-            parts.append(lax.dynamic_slice_in_dim(part_1, place * WIDTHS[1], WIDTHS[1], 1))
-        return jnp.concatenate(parts, axis=1)
+        places = (x, (x + 2) & 3)
+        starts = [(first, (place * 2 + half) * HALF, HALF) for place in places]
+        starts += [(part_1, place * WIDTHS[1], WIDTHS[1]) for place in places]
+        return jnp.concatenate([lax.dynamic_slice_in_dim(a, i, n, 1) for a, i, n in starts], axis=1)
 
     keep, give = column_block(core), column_block(1 - core)
     near = lax.ppermute(give, ALL, CORE_SWAP)
@@ -281,7 +278,10 @@
 
     spread_in = frames.reshape(2, HALO, 2, HALF).transpose(2, 1, 0, 3).reshape(256, 2, HALF)
     plane, spread_in = lax.optimization_barrier((plane, spread_in))
-    columns = lax.all_gather(plane, "gy", axis=0, tiled=True, axis_index_groups=Z_GROUPS)
+    columns_0, columns_1 = (
+        lax.all_gather(part, "gy", axis=0, tiled=True, axis_index_groups=Z_GROUPS)
+        for part in (plane[:, : 2 * WIDTHS[0]], plane[:, 2 * WIDTHS[0] :])
+    )
     spread = lax.all_to_all(spread_in, ALL, 0, 0, tiled=True).reshape(512, HALF)
 
     partner_0, partner_1 = matchings[0], matchings[1]
@@ -304,15 +304,15 @@
     ).reshape(-1)
     chosen = (wanted[:, None] == jnp.arange(512, dtype=jnp.int32)[None, :]).astype(jnp.bfloat16)
     routed = jnp.dot(chosen, spread, preferred_element_type=jnp.float32).astype(jnp.bfloat16)
-    columns, _ = lax.optimization_barrier((columns, routed))
+    columns_0, _ = lax.optimization_barrier((columns_0, routed))
     collected = lax.all_to_all(routed.reshape(256, 8, HALF), ALL, 0, 0, tiled=True)
     collected = collected.reshape(2048, HALF)
 
-    yours = lax.ppermute(columns, ALL, CORE_SWAP)
-    near_0 = next_to(columns[:, : WIDTHS[0]])
-    mine_0, yours_0 = (columns, *near_0), (yours, *other_core(near_0))
-    block_1, near_0 = lax.optimization_barrier((columns[:, WIDTHS[0] : GATHERED], near_0))
-    near_1 = next_to(block_1)
+    near_0 = next_to(columns_0[:, : WIDTHS[0]])
+    mine_0 = (columns_0, *near_0)
+    yours_0 = other_core(mine_0)
+    columns_1, near_0 = lax.optimization_barrier((columns_1, near_0))
+    near_1 = next_to(columns_1[:, : WIDTHS[1]])
 
     scal = jnp.stack([here, core, x]).astype(jnp.int32)
     run = functools.partial(layer, scal, lengths, matchings)
@@ -321,7 +321,8 @@
     own_tail = lax.dynamic_slice_in_dim(hidden, tail_start, HALO, 0)
     tail = lax.ppermute(own_tail, ALL, [(i, i + 1) for i in range(255)])
     near_1, hidden = lax.optimization_barrier((near_1, hidden))
-    mine_1, yours_1 = (columns, *near_1), (yours, *other_core(near_1))
+    mine_1 = (columns_1, *near_1)
+    yours_1 = other_core(mine_1)
     hidden_1 = run(mine_0, yours_0, (collected,), False, True)
     context = run(mine_1, yours_1, (hidden, hidden_1, tail), True, False)
     return hidden, context

time: 282 us -> 262 us (0.929)
  waiting for transfers between devices: 142 us -> 109 us
  starting transfers between devices: 42.9 us -> 56.2 us
    ppermute x4, waiting for transfers between devices: 67.7 us -> 48.5 us  [next_to(): return (lax.ppermute(block, ALL, X_DOWN), lax.ppermute(block, ALL, X_UP))]
    ppermute x4 -> x6, starting transfers between devices: 3.84 us -> 18.3 us  [other_core(): return tuple((lax.ppermute(piece, ALL, CORE_SWAP) for piece in pieces))]
    all_gather x1 -> x2, waiting for transfers between devices: 36.5 us -> 22.2 us  [local(): lax.all_gather(part, 'gy', axis=0, tiled=True, axis_index_groups=Z_GROUPS)]
    all_to_all x1, starting transfers between devices: 9.9 us -> 5.19 us  [local(): lax.all_to_all(routed.reshape(256, 8, HALF), ALL, 0, 0, tiled=True)]
    ppermute x4, starting transfers between devices: 4.14 us -> 7.96 us  [next_to(): return (lax.ppermute(block, ALL, X_DOWN), lax.ppermute(block, ALL, X_UP))]
  transfers between devices with their start and end apart: 16 -> 18, of which waited for: 7 -> 7; matrix products, arithmetic and copies ran while one was open for 4% -> 5% of each run, Pallas kernels for 15% -> 16%
where the time goes in v1:
time: 262 us
  waiting for transfers between devices  109 us (42%)
  Pallas kernels  59.9 us (23%)
  starting transfers between devices  56.2 us (21%)
  local copies, waits for them, and re-layouts  15.9 us (6%)
  between operations  15.1 us (6%)
  matrix products  3.28 us (1%)
    pallas_call x3, Pallas kernels, layer(): pl.pallas_call(functools.partial(layer_kernel, first_block, with_out), gr...  59.9 us
    ppermute x4, waiting for transfers between devices, next_to(): return (lax.ppermute(block, ALL, X_DOWN), lax.ppermute(block, ALL, X_UP))  48.5 us
    all_to_all x1, waiting for transfers between devices, local(): spread = lax.all_to_all(spread_in, ALL, 0, 0, tiled=True).reshape(512, HALF)  30.2 us
    all_gather x2, waiting for transfers between devices, local(): lax.all_gather(part, 'gy', axis=0, tiled=True, axis_index_groups=Z_GROUPS)  22.2 us
    ppermute x6, starting transfers between devices, other_core(): return tuple((lax.ppermute(piece, ALL, CORE_SWAP) for piece in pieces))  18.3 us
    all_to_all x1, starting transfers between devices, local(): spread = lax.all_to_all(spread_in, ALL, 0, 0, tiled=True).reshape(512, HALF)  13.2 us
    ppermute x1, waiting for transfers between devices, gather_rows(): cross = lax.ppermute(keep, ALL, CROSS_SWAP)  8.08 us
    ppermute x4, starting transfers between devices, next_to(): return (lax.ppermute(block, ALL, X_DOWN), lax.ppermute(block, ALL, X_UP))  7.96 us
  transfers between devices with their start and end apart: 18, of which 7 were waited for; matrix products, arithmetic and copies ran while one was open for 5% of the time, Pallas kernels for 16%

profile of v1, /device:TPU:1, one launch (start us, length us, event | category | flops | bytes accessed | tf_op | source)
XLA Modules:
  0.0 261.7 jit_solution(12312123606587578711)
XLA Ops:
  7.2 0.0 all-gather.5.cloned.1.call-start
  7.2 1.1 slice_bitcast_fusion
  8.4 0.1 reshape_squeeze.3
  8.5 0.0 copy-start.1
  8.5 2.0 dynamic-slice_reduce_fusion.1
  10.5 0.2 fusion.4
  10.7 3.3 %collective-permute-start = (bf16[40,2304]{1,0:T(8,128)(2,1)S(1)}, bf16[40,2304]{1,0:T(8,128)(2,1)S(1)}, u32[]{:S(2)}, u32[]{:S(2)}) collective-permute-start(bf16[40,2304]{1,0:T(8,128)(2,1)S(1)} %pad_maximum_fusion.1), channel_id=1, source_target_pairs={{0,1},{1,0},{2,3},{3,2},{4,5},{5,4},{6,7},{7,6},{8,9},{9,8},{10,11... | collective-permute-start | bytes 552968 | tf_op jit(solution)/shard_map/ppermute | solution.py:257
  14.1 1.0 collective-permute-start.2
  15.1 1.8 collective-permute-start.1
  16.9 0.1 reshape.140
  17.0 0.1 copy.24
  17.1 0.0 collective-permute-done
  17.1 0.1 maximum_select_fusion.1
  17.2 0.0 copy-start.3
  17.2 0.0 copy-start.4
  17.2 8.1 %collective-permute-done.1 = bf16[40,2304]{1,0:T(8,128)(2,1)S(1)} collective-permute-done((bf16[40,2304]{1,0:T(8,128)(2,1)S(1)}, bf16[40,2304]{1,0:T(8,128)(2,1)S(1)}, u32[]{:S(2)}, u32[]{:S(2)}) %collective-permute-start.1) | collective-permute-done | bytes 184352 | tf_op jit(solution)/shard_map/ppermute | solution.py:258
  25.3 0.0 collective-permute-done.2
  25.3 0.1 maximum_select_fusion.2
  25.4 0.1 maximum_select_fusion
  25.5 0.8 slice.27
  26.3 0.0 all-gather.5.cloned.1.call-update
  26.4 0.7 fusion.7
  27.1 1.5 copy.26
  28.6 13.2 %all-to-all-start = ((bf16[256,2,640]{2,1,0:T(2,128)(2,1)}), bf16[256,2,640]{2,1,0:T(2,128)(2,1)S(1)}, u32[]{:S(2)}, u32[]{:S(2)}) async-start(bf16[256,2,640]{2,1,0:T(2,128)(2,1)} %copy.26), calls=%async_computation | async-start | bytes 1310720 | tf_op jit(solution)/shard_map/all_to_all | solution.py:285
  41.8 0.2 select_reduce_fusion.2
  42.0 0.2 select_reduce_fusion
  42.3 0.1 copy.25
  42.4 0.1 eq.81
  42.6 30.2 %all-to-all-done = bf16[256,2,640]{2,1,0:T(2,128)(2,1)S(1)} async-done(((bf16[256,2,640]{2,1,0:T(2,128)(2,1)}), bf16[256,2,640]{2,1,0:T(2,128)(2,1)S(1)}, u32[]{:S(2)}, u32[]{:S(2)}) %all-to-all-start) | async-done | bytes 655392 | tf_op jit(solution)/shard_map/all_to_all | solution.py:285
  72.7 0.2 reshape.142
  73.0 3.3 %fusion.1 = bf16[2048,640]{1,0:T(8,128)(2,1)} fusion(bf16[512,640]{1,0:T(8,128)(2,1)S(1)} %reshape.142, s32[2048]{0:T(1024)S(1)} %eq.81), kind=kOutput, calls=%fused_computation.2 | convolution fusion | flops 1344536576 | bytes 3284992 | tf_op jit(solution)/shard_map/dot_general | solution.py:306
  76.3 5.2 %all-to-all-start.1 = ((bf16[256,8,640]{2,1,0:T(8,128)(2,1)}), bf16[256,8,640]{2,1,0:T(8,128)(2,1)S(1)}, u32[]{:S(2)}, u32[]{:S(2)}) async-start(bf16[256,8,640]{2,1,0:T(8,128)(2,1)} %bitcast.32), calls=%async_computation.1 | async-start | bytes 5242880 | tf_op jit(solution)/shard_map/all_to_all | solution.py:308
  81.4 0.0 all-gather.3.cloned.1.call-start
  81.5 0.8 slice.26
  82.3 0.0 all-gather.3.cloned.1.call-update
  82.3 13.2 %all-gather.5.cloned.1.call-done.refs_0_ = bf16[1280,1280]{1,0:T(8,128)(2,1)} async-done(((bf16[160,1280]{1,0:T(8,128)(2,1)}), bf16[1280,1280]{1,0:T(8,128)(2,1)}) %all-gather.5.cloned.1.call-update) | async-done | bytes 3276816 | tf_op jit(solution)/shard_map/all_gather | solution.py:282
  95.4 1.6 slice.30
  97.0 5.6 %collective-permute-start.3 = (bf16[1280,640]{1,0:T(8,128)(2,1)S(1)}, bf16[1280,640]{1,0:T(8,128)(2,1)}, u32[]{:S(2)}, u32[]{:S(2)}) collective-permute-start(bf16[1280,640]{1,0:T(8,128)(2,1)S(1)} %slice.30), channel_id=1, source_target_pairs={{0,192},{1,193},{2,194},{3,195},{4,196},{5,197},{6,198},{7,199},{8... | collective-permute-start | bytes 4915208 | tf_op jit(solution)/shard_map/ppermute | solution.py:237
  102.6 0.0 collective-permute-start.4
  102.6 5.1 %collective-permute-start.7 = (bf16[1280,1280]{1,0:T(8,128)(2,1)}, bf16[1280,1280]{1,0:T(8,128)(2,1)}, u32[]{:S(2)}, u32[]{:S(2)}) collective-permute-start(bf16[1280,1280]{1,0:T(8,128)(2,1)} %all-gather.5.cloned.1.call-done.refs_0_), channel_id=1, source_target_pairs={{0,1},{1,0},{2,3},{3,2},{4,5},{5,4},{6,7},{7,6},{8,9},{9,8},{10,11... | collective-permute-start | bytes 9830408 | tf_op jit(solution)/shard_map/ppermute | solution.py:241
  107.7 43.8 %collective-permute-done.3.refs_1_ = bf16[1280,640]{1,0:T(8,128)(2,1)} collective-permute-done((bf16[1280,640]{1,0:T(8,128)(2,1)S(1)}, bf16[1280,640]{1,0:T(8,128)(2,1)}, u32[]{:S(2)}, u32[]{:S(2)}) %collective-permute-start.3) | collective-permute-done | bytes 1638432 | tf_op jit(solution)/shard_map/ppermute | solution.py:237
  151.6 4.3 %collective-permute-start.8 = (bf16[1280,640]{1,0:T(8,128)(2,1)}, bf16[1280,640]{1,0:T(8,128)(2,1)}, u32[]{:S(2)}, u32[]{:S(2)}) collective-permute-start(bf16[1280,640]{1,0:T(8,128)(2,1)} %collective-permute-done.3.refs_1_), channel_id=1, source_target_pairs={{0,1},{1,0},{2,3},{3,2},{4,5},{5,4},{6,7},{7,6},{8,9},{9,8},{10,11... | collective-permute-start | bytes 4915208 | tf_op jit(solution)/shard_map/ppermute | solution.py:241
  155.9 3.6 %collective-permute-start.9 = (bf16[1280,640]{1,0:T(8,128)(2,1)}, bf16[1280,640]{1,0:T(8,128)(2,1)}, u32[]{:S(2)}, u32[]{:S(2)}) collective-permute-start(bf16[1280,640]{1,0:T(8,128)(2,1)} %collective-permute-done.4.refs_2_), channel_id=1, source_target_pairs={{0,1},{1,0},{2,3},{3,2},{4,5},{5,4},{6,7},{7,6},{8,9},{9,8},{10,11... | collective-permute-start | bytes 4915208 | tf_op jit(solution)/shard_map/ppermute | solution.py:241
  159.5 9.1 %all-gather.3.cloned.1.call-done.refs_0_ = bf16[1280,1024]{1,0:T(8,128)(2,1)} async-done(((bf16[160,1024]{1,0:T(8,128)(2,1)}), bf16[1280,1024]{1,0:T(8,128)(2,1)}) %all-gather.3.cloned.1.call-update) | async-done | bytes 2621456 | tf_op jit(solution)/shard_map/all_gather | solution.py:282
  168.5 2.5 slice.31
  171.0 2.4 collective-permute-start.5
  173.4 2.2 collective-permute-start.10
  175.6 0.6 pad_add_fusion.scal
  176.2 0.0 all-to-all-done.1
  176.2 0.0 collective-permute-done.9.refs_5_
  176.2 1.5 copy-done
  177.7 20.6 %shard_map.68.refs_6_ = bf16[256,1280]{1,0:T(8,128)(2,1)} custom-call(s32[3]{0:T(128)} %pad_add_fusion.scal, s32[256]{0:T(256)} %lengths.5, s32[2,256]{1,0:T(2,128)} %matchings.5, bf16[1280,1280]{1,0:T(8,128)(2,1)} %all-gather.5.cloned.1.call-done.refs_0_, bf16[1280,640]{1,0:T(8,128)(2,1)} %collective-permute-done.3.refs_1_, ...), custom_call_target="tpu_custom_call" | custom-call | flops 8000000000 | bytes 14000000 | tf_op jit(solution)/shard_map/pallas_call | solution.py:217
  198.3 1.6 collective-permute-done.5.refs_1_
  199.9 3.1 %collective-permute-done.6.refs_2_ = bf16[1280,512]{1,0:T(8,128)(2,1)} collective-permute-done((bf16[1280,512]{1,0:T(8,128)(2,1)}, bf16[1280,512]{1,0:T(8,128)(2,1)}, u32[]{:S(2)}, u32[]{:S(2)}) %collective-permute-start.6) | collective-permute-done | bytes 1310752 | tf_op jit(solution)/shard_map/ppermute | solution.py:237
  203.0 3.1 %collective-permute-start.11 = (bf16[1280,512]{1,0:T(8,128)(2,1)}, bf16[1280,512]{1,0:T(8,128)(2,1)S(1)}, u32[]{:S(2)}, u32[]{:S(2)}) collective-permute-start(bf16[1280,512]{1,0:T(8,128)(2,1)} %collective-permute-done.5.refs_1_), channel_id=1, source_target_pairs={{0,1},{1,0},{2,3},{3,2},{4,5},{5,4},{6,7},{7,6},{8,9},{9,8},{10,11... | collective-permute-start | bytes 3932168 | tf_op jit(solution)/shard_map/ppermute | solution.py:241
  206.1 0.0 collective-permute-start.12
  206.8 1.1 constant_dynamic-slice_fusion
  207.9 5.4 %collective-permute-start.13 = (bf16[128,1280]{1,0:T(8,128)(2,1)S(1)}, bf16[128,1280]{1,0:T(8,128)(2,1)S(1)}, u32[]{:S(2)}, u32[]{:S(2)}) collective-permute-start(bf16[128,1280]{1,0:T(8,128)(2,1)S(1)} %constant_dynamic-slice_fusion), channel_id=1, source_target_pairs={{0,1},{1,2},{2,3},{3,4},{4,5},{5,6},{6,7},{7,8},{8,9},{9,10},{10,1... | collective-permute-start | bytes 983048 | tf_op jit(solution)/shard_map/ppermute | solution.py:322
  213.3 20.7 %shard_map.69.refs_7_ = bf16[256,1280]{1,0:T(8,128)(2,1)} custom-call(s32[3]{0:T(128)} %pad_add_fusion.scal, s32[256]{0:T(256)} %lengths.5, s32[2,256]{1,0:T(2,128)} %matchings.5, bf16[1280,1280]{1,0:T(8,128)(2,1)} %all-gather.5.cloned.1.call-done.refs_0_, bf16[1280,640]{1,0:T(8,128)(2,1)} %collective-permute-done.3.refs_1_, ...), custom_call_target="tpu_custom_call" | custom-call | flops 8000000000 | bytes 14000000 | tf_op jit(solution)/shard_map/pallas_call | solution.py:217
  234.0 0.0 collective-permute-done.13.refs_8_
  234.1 0.7 copy-done.7
  234.7 0.4 copy-done.5
  235.2 1.0 copy-done.6
  236.2 18.6 %shard_map.70 = bf16[256,1280]{1,0:T(8,128)(2,1)} custom-call(s32[3]{0:T(128)} %pad_add_fusion.scal, s32[256]{0:T(256)} %lengths.5, s32[2,256]{1,0:T(2,128)} %matchings.5, bf16[1280,1024]{1,0:T(8,128)(2,1)} %all-gather.3.cloned.1.call-done.refs_0_, bf16[1280,512]{1,0:T(8,128)(2,1)} %collective-permute-done.5.refs_1_, ...), custom_call_target="tpu_custom_call" | custom-call | flops 8000000000 | bytes 14000000 | tf_op jit(solution)/shard_map/pallas_call | solution.py:217
  (30 shorter events, 0.2 us)
Async XLA Ops:
  7.2 88.3 %all-gather.5.cloned.1.call-start = ((), (), s32[]{:S(2)}) async-start(), calls=%async_computation.3 | async-start | bytes 3686400 | tf_op jit(solution)/shard_map/all_gather | solution.py:282
  7.2 3.3 %copy-start.2 = (bf16[1,40,1280]{2,1,0:T(8,128)(2,1)S(1)}, bf16[1,40,1280]{2,1,0:T(8,128)(2,1)}, u32[]{:S(2)}) copy-start(bf16[1,40,1280]{2,1,0:T(8,128)(2,1)} %param.9) | copy-start | bytes 307204
  8.5 8.4 %copy-start.1 = (bf16[256,1280]{1,0:T(8,128)(2,1)S(1)}, bf16[256,1280]{1,0:T(8,128)(2,1)}, u32[]{:S(2)}) copy-start(bf16[256,1280]{1,0:T(8,128)(2,1)} %refs_6_.1) | copy-start | bytes 1966084
  10.7 6.4 %collective-permute-start = (bf16[40,2304]{1,0:T(8,128)(2,1)S(1)}, bf16[40,2304]{1,0:T(8,128)(2,1)S(1)}, u32[]{:S(2)}, u32[]{:S(2)}) collective-permute-start(bf16[40,2304]{1,0:T(8,128)(2,1)S(1)} %pad_maximum_fusion.1), channel_id=1, source_target_pairs={{0,1},{1,0},{2,3},{3,2},{4,5},{5,4},{6,7},{7,6},{8,9},{9,8},{10,11... | collective-permute-start | bytes 552968 | tf_op jit(solution)/shard_map/ppermute | solution.py:257
  14.1 11.3 %collective-permute-start.2 = (bf16[40,2304]{1,0:T(8,128)(2,1)S(1)}, bf16[40,2304]{1,0:T(8,128)(2,1)S(1)}, u32[]{:S(2)}, u32[]{:S(2)}) collective-permute-start(bf16[40,2304]{1,0:T(8,128)(2,1)S(1)} %pad_maximum_fusion.1), channel_id=1, source_target_pairs={{0,35},{1,34},{2,33},{3,32},{4,39},{5,38},{6,37},{7,36},{8,43},{9,... | collective-permute-start | bytes 552968 | tf_op jit(solution)/shard_map/ppermute | solution.py:259
  15.1 10.2 %collective-permute-start.1 = (bf16[40,2304]{1,0:T(8,128)(2,1)S(1)}, bf16[40,2304]{1,0:T(8,128)(2,1)S(1)}, u32[]{:S(2)}, u32[]{:S(2)}) collective-permute-start(bf16[40,2304]{1,0:T(8,128)(2,1)S(1)} %pad_maximum_fusion), channel_id=1, source_target_pairs={{0,34},{1,35},{2,32},{3,33},{4,38},{5,39},{6,36},{7,37},{8,42},{9,... | collective-permute-start | bytes 552968 | tf_op jit(solution)/shard_map/ppermute | solution.py:258
  17.2 9.1 %copy-start.3 = (s32[2,256]{1,0:T(2,128)S(1)}, s32[2,256]{1,0:T(2,128)}, u32[]{:S(2)}) copy-start(s32[2,256]{1,0:T(2,128)} %matchings.5) | copy-start | bytes 6148
  17.2 9.1 %copy-start.4 = (s32[256]{0:T(256)S(1)}, s32[256]{0:T(256)}, u32[]{:S(2)}) copy-start(s32[256]{0:T(256)} %lengths.5) | copy-start | bytes 3076
  28.6 44.1 %all-to-all-start = ((bf16[256,2,640]{2,1,0:T(2,128)(2,1)}), bf16[256,2,640]{2,1,0:T(2,128)(2,1)S(1)}, u32[]{:S(2)}, u32[]{:S(2)}) async-start(bf16[256,2,640]{2,1,0:T(2,128)(2,1)} %copy.26), calls=%async_computation | async-start | bytes 1310720 | tf_op jit(solution)/shard_map/all_to_all | solution.py:285
  76.3 100.0 %all-to-all-start.1 = ((bf16[256,8,640]{2,1,0:T(8,128)(2,1)}), bf16[256,8,640]{2,1,0:T(8,128)(2,1)S(1)}, u32[]{:S(2)}, u32[]{:S(2)}) async-start(bf16[256,8,640]{2,1,0:T(8,128)(2,1)} %bitcast.32), calls=%async_computation.1 | async-start | bytes 5242880 | tf_op jit(solution)/shard_map/all_to_all | solution.py:308
  81.4 87.1 %all-gather.3.cloned.1.call-start = ((), (), s32[]{:S(2)}) async-start(), calls=%async_computation.2 | async-start | bytes 2949120 | tf_op jit(solution)/shard_map/all_gather | solution.py:282
  97.0 54.5 %collective-permute-start.3 = (bf16[1280,640]{1,0:T(8,128)(2,1)S(1)}, bf16[1280,640]{1,0:T(8,128)(2,1)}, u32[]{:S(2)}, u32[]{:S(2)}) collective-permute-start(bf16[1280,640]{1,0:T(8,128)(2,1)S(1)} %slice.30), channel_id=1, source_target_pairs={{0,192},{1,193},{2,194},{3,195},{4,196},{5,197},{6,198},{7,199},{8... | collective-permute-start | bytes 4915208 | tf_op jit(solution)/shard_map/ppermute | solution.py:237
  102.6 53.3 %collective-permute-start.4 = (bf16[1280,640]{1,0:T(8,128)(2,1)S(1)}, bf16[1280,640]{1,0:T(8,128)(2,1)}, u32[]{:S(2)}, u32[]{:S(2)}) collective-permute-start(bf16[1280,640]{1,0:T(8,128)(2,1)S(1)} %slice.30), channel_id=1, source_target_pairs={{0,64},{1,65},{2,66},{3,67},{4,68},{5,69},{6,70},{7,71},{8,72},{9,... | collective-permute-start | bytes 4915208 | tf_op jit(solution)/shard_map/ppermute | solution.py:237
  102.6 73.6 %collective-permute-start.7 = (bf16[1280,1280]{1,0:T(8,128)(2,1)}, bf16[1280,1280]{1,0:T(8,128)(2,1)}, u32[]{:S(2)}, u32[]{:S(2)}) collective-permute-start(bf16[1280,1280]{1,0:T(8,128)(2,1)} %all-gather.5.cloned.1.call-done.refs_0_), channel_id=1, source_target_pairs={{0,1},{1,0},{2,3},{3,2},{4,5},{5,4},{6,7},{7,6},{8,9},{9,8},{10,11... | collective-permute-start | bytes 9830408 | tf_op jit(solution)/shard_map/ppermute | solution.py:241
  151.6 21.8 %collective-permute-start.8 = (bf16[1280,640]{1,0:T(8,128)(2,1)}, bf16[1280,640]{1,0:T(8,128)(2,1)}, u32[]{:S(2)}, u32[]{:S(2)}) collective-permute-start(bf16[1280,640]{1,0:T(8,128)(2,1)} %collective-permute-done.3.refs_1_), channel_id=1, source_target_pairs={{0,1},{1,0},{2,3},{3,2},{4,5},{5,4},{6,7},{7,6},{8,9},{9,8},{10,11... | collective-permute-start | bytes 4915208 | tf_op jit(solution)/shard_map/ppermute | solution.py:241
  155.9 20.3 %collective-permute-start.9 = (bf16[1280,640]{1,0:T(8,128)(2,1)}, bf16[1280,640]{1,0:T(8,128)(2,1)}, u32[]{:S(2)}, u32[]{:S(2)}) collective-permute-start(bf16[1280,640]{1,0:T(8,128)(2,1)} %collective-permute-done.4.refs_2_), channel_id=1, source_target_pairs={{0,1},{1,0},{2,3},{3,2},{4,5},{5,4},{6,7},{7,6},{8,9},{9,8},{10,11... | collective-permute-start | bytes 4915208 | tf_op jit(solution)/shard_map/ppermute | solution.py:241
  171.0 28.8 %collective-permute-start.5 = (bf16[1280,512]{1,0:T(8,128)(2,1)}, bf16[1280,512]{1,0:T(8,128)(2,1)}, u32[]{:S(2)}, u32[]{:S(2)}) collective-permute-start(bf16[1280,512]{1,0:T(8,128)(2,1)} %slice.31), channel_id=1, source_target_pairs={{0,192},{1,193},{2,194},{3,195},{4,196},{5,197},{6,198},{7,199},{8... | collective-permute-start | bytes 3932168 | tf_op jit(solution)/shard_map/ppermute | solution.py:237
  173.4 29.6 %collective-permute-start.6 = (bf16[1280,512]{1,0:T(8,128)(2,1)}, bf16[1280,512]{1,0:T(8,128)(2,1)}, u32[]{:S(2)}, u32[]{:S(2)}) collective-permute-start(bf16[1280,512]{1,0:T(8,128)(2,1)} %slice.31), channel_id=1, source_target_pairs={{0,64},{1,65},{2,66},{3,67},{4,68},{5,69},{6,70},{7,71},{8,72},{9,... | collective-permute-start | bytes 3932168 | tf_op jit(solution)/shard_map/ppermute | solution.py:237
  173.4 60.6 %collective-permute-start.10 = (bf16[1280,1024]{1,0:T(8,128)(2,1)}, bf16[1280,1024]{1,0:T(8,128)(2,1)}, u32[]{:S(2)}, u32[]{:S(2)}) collective-permute-start(bf16[1280,1024]{1,0:T(8,128)(2,1)} %all-gather.3.cloned.1.call-done.refs_0_), channel_id=1, source_target_pairs={{0,1},{1,0},{2,3},{3,2},{4,5},{5,4},{6,7},{7,6},{8,9},{9,8},{10,11... | collective-permute-start | bytes 7864328 | tf_op jit(solution)/shard_map/ppermute | solution.py:241
  176.2 1.5 copy-start
  203.0 31.0 %collective-permute-start.11 = (bf16[1280,512]{1,0:T(8,128)(2,1)}, bf16[1280,512]{1,0:T(8,128)(2,1)S(1)}, u32[]{:S(2)}, u32[]{:S(2)}) collective-permute-start(bf16[1280,512]{1,0:T(8,128)(2,1)} %collective-permute-done.5.refs_1_), channel_id=1, source_target_pairs={{0,1},{1,0},{2,3},{3,2},{4,5},{5,4},{6,7},{7,6},{8,9},{9,8},{10,11... | collective-permute-start | bytes 3932168 | tf_op jit(solution)/shard_map/ppermute | solution.py:241
  206.1 27.9 %collective-permute-start.12 = (bf16[1280,512]{1,0:T(8,128)(2,1)}, bf16[1280,512]{1,0:T(8,128)(2,1)S(1)}, u32[]{:S(2)}, u32[]{:S(2)}) collective-permute-start(bf16[1280,512]{1,0:T(8,128)(2,1)} %collective-permute-done.6.refs_2_), channel_id=1, source_target_pairs={{0,1},{1,0},{2,3},{3,2},{4,5},{5,4},{6,7},{7,6},{8,9},{9,8},{10,11... | collective-permute-start | bytes 3932168 | tf_op jit(solution)/shard_map/ppermute | solution.py:241
  207.9 26.1 %collective-permute-start.13 = (bf16[128,1280]{1,0:T(8,128)(2,1)S(1)}, bf16[128,1280]{1,0:T(8,128)(2,1)S(1)}, u32[]{:S(2)}, u32[]{:S(2)}) collective-permute-start(bf16[128,1280]{1,0:T(8,128)(2,1)S(1)} %constant_dynamic-slice_fusion), channel_id=1, source_target_pairs={{0,1},{1,2},{2,3},{3,4},{4,5},{5,6},{6,7},{7,8},{8,9},{9,10},{10,1... | collective-permute-start | bytes 983048 | tf_op jit(solution)/shard_map/ppermute | solution.py:322
  234.0 0.7 copy-start.7
  234.0 1.2 copy-start.5
  235.2 1.1 copy-start.6
Sparse Core Ops, SparseCore 0:
  26.4 68.9 all-gather.4
  97.8 70.6 all-gather.2

commit v2 on v1

--- a/solution.py
+++ b/solution.py
@@ -241,17 +241,16 @@
     return tuple(lax.ppermute(piece, ALL, CORE_SWAP) for piece in pieces)
 
 
-def gather_rows(wqkv, wout, x, core, y_hi):
-    first = jnp.concatenate([wqkv[0], wout[0]], axis=1)
-    second = wqkv[1].reshape(-1, 3, 2, HALF)
-
+def gather_rows(weights, width, x, core, y_hi):
     def column_block(half):
-        part_1 = lax.dynamic_index_in_dim(second, half, 2, keepdims=False).reshape(-1, 3 * HALF)
-        part_1 = jnp.pad(part_1, ((0, 0), (0, 128)))
-        places = (x, (x + 2) & 3)
-        starts = [(first, (place * 2 + half) * HALF, HALF) for place in places]
-        starts += [(part_1, place * WIDTHS[1], WIDTHS[1]) for place in places]
-        return jnp.concatenate([lax.dynamic_slice_in_dim(a, i, n, 1) for a, i, n in starts], axis=1)
+        columns = weights(half)
+        return jnp.concatenate(
+            [
+                lax.dynamic_slice_in_dim(columns, place * width, width, 1)
+                for place in (x, (x + 2) & 3)
+            ],
+            axis=1,
+        )
 
     keep, give = column_block(core), column_block(1 - core)
     near = lax.ppermute(give, ALL, CORE_SWAP)
@@ -274,13 +273,25 @@
     gx, gy = lax.axis_index("gx"), lax.axis_index("gy")
     here = gx * 32 + gy
     core, y_hi, x = gy & 1, (gy >> 1) & 1, gx >> 1
-    plane = gather_rows(wqkv, wout, x, core, y_hi)
+
+    def half_0(half):
+        columns = jnp.concatenate([wqkv[0], wout[0]], axis=1).reshape(-1, 4, 2, HALF)
+        return lax.dynamic_index_in_dim(columns, half, 2, keepdims=False).reshape(-1, 4 * HALF)
+
+    plane_0 = gather_rows(half_0, WIDTHS[0], x, core, y_hi)
 
     spread_in = frames.reshape(2, HALO, 2, HALF).transpose(2, 1, 0, 3).reshape(256, 2, HALF)
-    plane, spread_in = lax.optimization_barrier((plane, spread_in))
+    plane_0, spread_in, wqkv_1 = lax.optimization_barrier((plane_0, spread_in, wqkv[1]))
+
+    def half_1(half):
+        columns = wqkv_1.reshape(-1, 3, 2, HALF)
+        columns = lax.dynamic_index_in_dim(columns, half, 2, keepdims=False).reshape(-1, 3 * HALF)
+        return jnp.pad(columns, ((0, 0), (0, 4 * WIDTHS[1] - 3 * HALF)))
+
+    plane_1 = gather_rows(half_1, WIDTHS[1], x, core, y_hi)
     columns_0, columns_1 = (
         lax.all_gather(part, "gy", axis=0, tiled=True, axis_index_groups=Z_GROUPS)
-        for part in (plane[:, : 2 * WIDTHS[0]], plane[:, 2 * WIDTHS[0] :])
+        for part in (plane_0, plane_1)
     )
     spread = lax.all_to_all(spread_in, ALL, 0, 0, tiled=True).reshape(512, HALF)
 
@@ -320,10 +331,10 @@
     tail_start = jnp.maximum(lookup(lengths, here) - HALO, 0)
     own_tail = lax.dynamic_slice_in_dim(hidden, tail_start, HALO, 0)
     tail = lax.ppermute(own_tail, ALL, [(i, i + 1) for i in range(255)])
-    near_1, hidden = lax.optimization_barrier((near_1, hidden))
-    mine_1 = (columns_1, *near_1)
-    yours_1 = other_core(mine_1)
+    far_1 = other_core((columns_1,))
     hidden_1 = run(mine_0, yours_0, (collected,), False, True)
+    near_1, hidden, hidden_1 = lax.optimization_barrier((near_1, hidden, hidden_1))
+    mine_1, yours_1 = (columns_1, *near_1), (*far_1, *other_core(near_1))
     context = run(mine_1, yours_1, (hidden, hidden_1, tail), True, False)
     return hidden, context
 

time: 262 us -> 259 us (0.989); the launches traced: 262 us -> 255 us
  waiting for transfers between devices: 109 us -> 96.6 us
    all_gather x2, waiting for transfers between devices: 22.2 us -> 9.49 us  [local(): lax.all_gather(part, 'gy', axis=0, tiled=True, axis_index_groups=Z_GROUPS)]
    ppermute x4, waiting for transfers between devices: 48.5 us -> 43.5 us  [next_to(): return (lax.ppermute(block, ALL, X_DOWN), lax.ppermute(block, ALL, X_UP))]
    ppermute x1, waiting for transfers between devices: 0.01 us -> 3.74 us  [local(): tail = lax.ppermute(own_tail, ALL, [(i, i + 1) for i in range(255)])]
    ppermute x1 -> x2, waiting for transfers between devices: 8.08 us -> 11.8 us  [gather_rows(): cross = lax.ppermute(keep, ALL, CROSS_SWAP)]
  transfers between devices with their start and end apart: 18 -> 21, of which waited for: 7 -> 7; matrix products, arithmetic and copies ran while one was open for 5% -> 6% of each run, Pallas kernels for 16% -> 16%
where the time goes in v2:
time: 259 us; the launch traced here: 255 us
  waiting for transfers between devices  96.6 us (37%)
  Pallas kernels  60 us (23%)
  starting transfers between devices  58.6 us (23%)
  local copies, waits for them, and re-layouts  17.4 us (7%)
  between operations  15 us (6%)
  other arithmetic  4.4 us (2%)
  matrix products  3.28 us (1%)
    pallas_call x3, Pallas kernels, layer(): pl.pallas_call(functools.partial(layer_kernel, first_block, with_out), gr...  60 us
    ppermute x4, waiting for transfers between devices, next_to(): return (lax.ppermute(block, ALL, X_DOWN), lax.ppermute(block, ALL, X_UP))  43.5 us
    all_to_all x1, waiting for transfers between devices, local(): spread = lax.all_to_all(spread_in, ALL, 0, 0, tiled=True).reshape(512, HALF)  28 us
    ppermute x6, starting transfers between devices, other_core(): return tuple((lax.ppermute(piece, ALL, CORE_SWAP) for piece in pieces))  16.2 us
    all_to_all x1, starting transfers between devices, local(): spread = lax.all_to_all(spread_in, ALL, 0, 0, tiled=True).reshape(512, HALF)  13.2 us
    ppermute x2, waiting for transfers between devices, gather_rows(): cross = lax.ppermute(keep, ALL, CROSS_SWAP)  11.8 us
    all_gather x2, waiting for transfers between devices, local(): lax.all_gather(part, 'gy', axis=0, tiled=True, axis_index_groups=Z_GROUPS)  9.49 us
    ppermute x4, starting transfers between devices, next_to(): return (lax.ppermute(block, ALL, X_DOWN), lax.ppermute(block, ALL, X_UP))  8.15 us
  transfers between devices with their start and end apart: 21, of which 7 were waited for; matrix products, arithmetic and copies ran while one was open for 6% of the time, Pallas kernels for 16%

profile of v2, /device:TPU:1, one launch (start us, length us, event | category | flops | bytes accessed | tf_op | source)
XLA Modules:
  0.0 255.4 jit_solution(18400242822948275088)
XLA Ops:
  7.2 0.0 all-gather.5.cloned.1.call-start
  7.2 0.0 copy-start.1
  7.2 1.2 slice_bitcast_fusion
  8.4 0.9 pad_maximum_fusion
  9.3 0.3 reshape.154
  9.6 2.6 dynamic-slice_reduce_fusion.1
  12.3 3.3 %collective-permute-start = (bf16[40,1280]{1,0:T(8,128)(2,1)S(1)}, bf16[40,1280]{1,0:T(8,128)(2,1)S(1)}, u32[]{:S(2)}, u32[]{:S(2)}) collective-permute-start(bf16[40,1280]{1,0:T(8,128)(2,1)S(1)} %pad_maximum_fusion.2), channel_id=1, source_target_pairs={{0,1},{1,0},{2,3},{3,2},{4,5},{5,4},{6,7},{7,6},{8,9},{9,8},{10,11... | collective-permute-start | bytes 307208 | tf_op jit(solution)/shard_map/ppermute | solution.py:256
  15.6 1.0 collective-permute-start.2
  16.6 0.0 copy-start.3
  16.6 0.0 copy-start.2
  16.7 1.8 collective-permute-start.1
  18.4 0.1 reshape.157
  18.6 0.1 copy.32
  18.7 0.0 collective-permute-done
  18.7 4.6 %collective-permute-done.1 = bf16[40,1280]{1,0:T(8,128)(2,1)S(1)} collective-permute-done((bf16[40,1280]{1,0:T(8,128)(2,1)S(1)}, bf16[40,1280]{1,0:T(8,128)(2,1)S(1)}, u32[]{:S(2)}, u32[]{:S(2)}) %collective-permute-start.1) | collective-permute-done | bytes 102432 | tf_op jit(solution)/shard_map/ppermute | solution.py:257
  23.3 0.0 collective-permute-done.2
  23.4 0.8 maximum_select_fusion
  24.2 0.0 all-gather.5.cloned.1.call-update
  24.3 0.6 fusion.3
  24.9 1.5 copy.36
  26.4 13.2 %all-to-all-start = ((bf16[256,2,640]{2,1,0:T(2,128)(2,1)}), bf16[256,2,640]{2,1,0:T(2,128)(2,1)S(1)}, u32[]{:S(2)}, u32[]{:S(2)}) async-start(bf16[256,2,640]{2,1,0:T(2,128)(2,1)} %copy.36), calls=%async_computation | async-start | bytes 1310720 | tf_op jit(solution)/shard_map/all_to_all | solution.py:296
  39.6 0.2 select_reduce_fusion.2
  39.8 0.3 select_reduce_fusion
  40.1 0.1 copy.35
  40.3 0.1 eq.84
  40.4 0.1 reshape.159
  40.5 2.0 dynamic-slice_reduce_fusion.3
  42.5 28.0 %all-to-all-done = bf16[256,2,640]{2,1,0:T(2,128)(2,1)S(1)} async-done(((bf16[256,2,640]{2,1,0:T(2,128)(2,1)}), bf16[256,2,640]{2,1,0:T(2,128)(2,1)S(1)}, u32[]{:S(2)}, u32[]{:S(2)}) %all-to-all-start) | async-done | bytes 655392 | tf_op jit(solution)/shard_map/all_to_all | solution.py:296
  70.6 0.2 reshape.162
  70.8 3.3 %fusion.1 = bf16[2048,640]{1,0:T(8,128)(2,1)} fusion(bf16[512,640]{1,0:T(8,128)(2,1)S(1)} %reshape.162, s32[2048]{0:T(1024)S(1)} %eq.84), kind=kOutput, calls=%fused_computation.2 | convolution fusion | flops 1344536576 | bytes 3284992 | tf_op jit(solution)/shard_map/dot_general | solution.py:317
  74.1 5.4 %all-to-all-start.1 = ((bf16[256,8,640]{2,1,0:T(8,128)(2,1)}), bf16[256,8,640]{2,1,0:T(8,128)(2,1)S(1)}, u32[]{:S(2)}, u32[]{:S(2)}) async-start(bf16[256,8,640]{2,1,0:T(8,128)(2,1)} %bitcast.38), calls=%async_computation.1 | async-start | bytes 5242880 | tf_op jit(solution)/shard_map/all_to_all | solution.py:319
  79.5 0.0 all-gather.3.cloned.1.call-start
  79.5 1.8 collective-permute-start.3
  81.3 0.9 collective-permute-start.5
  82.3 1.8 collective-permute-start.4
  84.1 0.0 collective-permute-done.3
  84.1 7.2 %collective-permute-done.4 = bf16[40,1024]{1,0:T(8,128)(2,1)S(1)} collective-permute-done((bf16[40,1024]{1,0:T(8,128)(2,1)S(1)}, bf16[40,1024]{1,0:T(8,128)(2,1)S(1)}, u32[]{:S(2)}, u32[]{:S(2)}) %collective-permute-start.4) | collective-permute-done | bytes 81952 | tf_op jit(solution)/shard_map/ppermute | solution.py:257
  91.4 0.8 maximum_select_fusion.1
  92.2 0.0 all-gather.3.cloned.1.call-update
  92.2 1.1 all-gather.5.cloned.1.call-done.refs_0_
  93.3 1.6 slice.23
  94.8 5.8 %collective-permute-start.6 = (bf16[1280,640]{1,0:T(8,128)(2,1)S(1)}, bf16[1280,640]{1,0:T(8,128)(2,1)}, u32[]{:S(2)}, u32[]{:S(2)}) collective-permute-start(bf16[1280,640]{1,0:T(8,128)(2,1)S(1)} %slice.23), channel_id=1, source_target_pairs={{0,192},{1,193},{2,194},{3,195},{4,196},{5,197},{6,198},{7,199},{8... | collective-permute-start | bytes 4915208 | tf_op jit(solution)/shard_map/ppermute | solution.py:237
  100.6 0.0 collective-permute-start.7
  100.6 5.2 %collective-permute-start.10 = (bf16[1280,1280]{1,0:T(8,128)(2,1)}, bf16[1280,1280]{1,0:T(8,128)(2,1)}, u32[]{:S(2)}, u32[]{:S(2)}) collective-permute-start(bf16[1280,1280]{1,0:T(8,128)(2,1)} %all-gather.5.cloned.1.call-done.refs_0_), channel_id=1, source_target_pairs={{0,1},{1,0},{2,3},{3,2},{4,5},{5,4},{6,7},{7,6},{8,9},{9,8},{10,11... | collective-permute-start | bytes 9830408 | tf_op jit(solution)/shard_map/ppermute | solution.py:241
  105.9 43.5 %collective-permute-done.6.refs_1_ = bf16[1280,640]{1,0:T(8,128)(2,1)} collective-permute-done((bf16[1280,640]{1,0:T(8,128)(2,1)S(1)}, bf16[1280,640]{1,0:T(8,128)(2,1)}, u32[]{:S(2)}, u32[]{:S(2)}) %collective-permute-start.6) | collective-permute-done | bytes 1638432 | tf_op jit(solution)/shard_map/ppermute | solution.py:237
  149.3 4.6 %collective-permute-start.11 = (bf16[1280,640]{1,0:T(8,128)(2,1)}, bf16[1280,640]{1,0:T(8,128)(2,1)}, u32[]{:S(2)}, u32[]{:S(2)}) collective-permute-start(bf16[1280,640]{1,0:T(8,128)(2,1)} %collective-permute-done.6.refs_1_), channel_id=1, source_target_pairs={{0,1},{1,0},{2,3},{3,2},{4,5},{5,4},{6,7},{7,6},{8,9},{9,8},{10,11... | collective-permute-start | bytes 4915208 | tf_op jit(solution)/shard_map/ppermute | solution.py:241
  153.9 3.6 %collective-permute-start.12 = (bf16[1280,640]{1,0:T(8,128)(2,1)}, bf16[1280,640]{1,0:T(8,128)(2,1)}, u32[]{:S(2)}, u32[]{:S(2)}) collective-permute-start(bf16[1280,640]{1,0:T(8,128)(2,1)} %collective-permute-done.7.refs_2_), channel_id=1, source_target_pairs={{0,1},{1,0},{2,3},{3,2},{4,5},{5,4},{6,7},{7,6},{8,9},{9,8},{10,11... | collective-permute-start | bytes 4915208 | tf_op jit(solution)/shard_map/ppermute | solution.py:241
  157.5 0.6 pad_add_fusion.scal
  158.0 8.4 %all-gather.3.cloned.1.call-done.refs_0_ = bf16[1280,1024]{1,0:T(8,128)(2,1)} async-done(((bf16[160,1024]{1,0:T(8,128)(2,1)}), bf16[1280,1024]{1,0:T(8,128)(2,1)}) %all-gather.3.cloned.1.call-update) | async-done | bytes 2621456 | tf_op jit(solution)/shard_map/all_gather | solution.py:293
  166.4 2.5 slice.24
  168.9 2.4 collective-permute-start.8
  171.3 2.2 collective-permute-start.13
  173.5 1.5 copy-done
  175.0 20.8 %shard_map.69.refs_7_ = bf16[256,1280]{1,0:T(8,128)(2,1)} custom-call(s32[3]{0:T(128)} %pad_add_fusion.scal, s32[256]{0:T(256)} %lengths.5, s32[2,256]{1,0:T(2,128)} %matchings.5, bf16[1280,1280]{1,0:T(8,128)(2,1)} %all-gather.5.cloned.1.call-done.refs_0_, bf16[1280,640]{1,0:T(8,128)(2,1)} %collective-permute-done.6.refs_1_, ...), custom_call_target="tpu_custom_call" | custom-call | flops 8000000000 | bytes 14000000 | tf_op jit(solution)/shard_map/pallas_call | solution.py:217
  195.8 20.7 %shard_map.68.refs_6_ = bf16[256,1280]{1,0:T(8,128)(2,1)} custom-call(s32[3]{0:T(128)} %pad_add_fusion.scal, s32[256]{0:T(256)} %lengths.5, s32[2,256]{1,0:T(2,128)} %matchings.5, bf16[1280,1280]{1,0:T(8,128)(2,1)} %all-gather.5.cloned.1.call-done.refs_0_, bf16[1280,640]{1,0:T(8,128)(2,1)} %collective-permute-done.6.refs_1_, ...), custom_call_target="tpu_custom_call" | custom-call | flops 8000000000 | bytes 14000000 | tf_op jit(solution)/shard_map/pallas_call | solution.py:217
  216.5 0.1 collective-permute-start.14
  216.6 0.5 collective-permute-start.15
  217.7 1.1 constant_dynamic-slice_fusion
  218.8 5.1 %collective-permute-start.16 = (bf16[128,1280]{1,0:T(8,128)(2,1)S(1)}, bf16[128,1280]{1,0:T(8,128)(2,1)S(1)}, u32[]{:S(2)}, u32[]{:S(2)}) collective-permute-start(bf16[128,1280]{1,0:T(8,128)(2,1)S(1)} %constant_dynamic-slice_fusion), channel_id=1, source_target_pairs={{0,1},{1,2},{2,3},{3,4},{4,5},{5,6},{6,7},{7,8},{8,9},{9,10},{10,1... | collective-permute-start | bytes 983048 | tf_op jit(solution)/shard_map/ppermute | solution.py:333
  223.9 3.7 %collective-permute-done.16.refs_8_ = bf16[128,1280]{1,0:T(8,128)(2,1)S(1)} collective-permute-done((bf16[128,1280]{1,0:T(8,128)(2,1)S(1)}, bf16[128,1280]{1,0:T(8,128)(2,1)S(1)}, u32[]{:S(2)}, u32[]{:S(2)}) %collective-permute-start.16) | collective-permute-done | bytes 327712 | tf_op jit(solution)/shard_map/ppermute | solution.py:333
  227.7 0.7 copy-done.6
  228.4 0.5 copy-done.4
  228.9 1.1 copy-done.5
  229.9 18.6 %shard_map.70 = bf16[256,1280]{1,0:T(8,128)(2,1)} custom-call(s32[3]{0:T(128)} %pad_add_fusion.scal, s32[256]{0:T(256)} %lengths.5, s32[2,256]{1,0:T(2,128)} %matchings.5, bf16[1280,1024]{1,0:T(8,128)(2,1)} %all-gather.3.cloned.1.call-done.refs_0_, bf16[1280,512]{1,0:T(8,128)(2,1)} %collective-permute-done.8.refs_1_, ...), custom_call_target="tpu_custom_call" | custom-call | flops 8000000000 | bytes 14000000 | tf_op jit(solution)/shard_map/pallas_call | solution.py:217
  (43 shorter events, 0.5 us)
Async XLA Ops:
  7.2 86.1 %all-gather.5.cloned.1.call-start = ((), (), s32[]{:S(2)}) async-start(), calls=%async_computation.3 | async-start | bytes 3686400 | tf_op jit(solution)/shard_map/all_gather | solution.py:293
  7.2 11.2 %copy-start.1 = (bf16[256,1280]{1,0:T(8,128)(2,1)S(1)}, bf16[256,1280]{1,0:T(8,128)(2,1)}, u32[]{:S(2)}) copy-start(bf16[256,1280]{1,0:T(8,128)(2,1)} %refs_6_.1) | copy-start | bytes 1966084
  12.3 6.4 %collective-permute-start = (bf16[40,1280]{1,0:T(8,128)(2,1)S(1)}, bf16[40,1280]{1,0:T(8,128)(2,1)S(1)}, u32[]{:S(2)}, u32[]{:S(2)}) collective-permute-start(bf16[40,1280]{1,0:T(8,128)(2,1)S(1)} %pad_maximum_fusion.2), channel_id=1, source_target_pairs={{0,1},{1,0},{2,3},{3,2},{4,5},{5,4},{6,7},{7,6},{8,9},{9,8},{10,11... | collective-permute-start | bytes 307208 | tf_op jit(solution)/shard_map/ppermute | solution.py:256
  15.6 7.7 %collective-permute-start.2 = (bf16[40,1280]{1,0:T(8,128)(2,1)S(1)}, bf16[40,1280]{1,0:T(8,128)(2,1)S(1)}, u32[]{:S(2)}, u32[]{:S(2)}) collective-permute-start(bf16[40,1280]{1,0:T(8,128)(2,1)S(1)} %pad_maximum_fusion.2), channel_id=1, source_target_pairs={{0,35},{1,34},{2,33},{3,32},{4,39},{5,38},{6,37},{7,36},{8,43},{9,... | collective-permute-start | bytes 307208 | tf_op jit(solution)/shard_map/ppermute | solution.py:258
  16.6 7.6 %copy-start.3 = (s32[256]{0:T(256)S(1)}, s32[256]{0:T(256)}, u32[]{:S(2)}) copy-start(s32[256]{0:T(256)} %lengths.5) | copy-start | bytes 3076
  16.6 8.3 %copy-start.2 = (s32[2,256]{1,0:T(2,128)S(1)}, s32[2,256]{1,0:T(2,128)}, u32[]{:S(2)}) copy-start(s32[2,256]{1,0:T(2,128)} %matchings.5) | copy-start | bytes 6148
  16.7 6.7 %collective-permute-start.1 = (bf16[40,1280]{1,0:T(8,128)(2,1)S(1)}, bf16[40,1280]{1,0:T(8,128)(2,1)S(1)}, u32[]{:S(2)}, u32[]{:S(2)}) collective-permute-start(bf16[40,1280]{1,0:T(8,128)(2,1)S(1)} %pad_maximum_fusion.1), channel_id=1, source_target_pairs={{0,34},{1,35},{2,32},{3,33},{4,38},{5,39},{6,36},{7,37},{8,42},{9,... | collective-permute-start | bytes 307208 | tf_op jit(solution)/shard_map/ppermute | solution.py:257
  26.4 44.1 %all-to-all-start = ((bf16[256,2,640]{2,1,0:T(2,128)(2,1)}), bf16[256,2,640]{2,1,0:T(2,128)(2,1)S(1)}, u32[]{:S(2)}, u32[]{:S(2)}) async-start(bf16[256,2,640]{2,1,0:T(2,128)(2,1)} %copy.36), calls=%async_computation | async-start | bytes 1310720 | tf_op jit(solution)/shard_map/all_to_all | solution.py:296
  74.1 99.4 %all-to-all-start.1 = ((bf16[256,8,640]{2,1,0:T(8,128)(2,1)}), bf16[256,8,640]{2,1,0:T(8,128)(2,1)S(1)}, u32[]{:S(2)}, u32[]{:S(2)}) async-start(bf16[256,8,640]{2,1,0:T(8,128)(2,1)} %bitcast.38), calls=%async_computation.1 | async-start | bytes 5242880 | tf_op jit(solution)/shard_map/all_to_all | solution.py:319
  79.5 87.0 %all-gather.3.cloned.1.call-start = ((), (), s32[]{:S(2)}) async-start(), calls=%async_computation.2 | async-start | bytes 2949120 | tf_op jit(solution)/shard_map/all_gather | solution.py:293
  79.5 4.6 %collective-permute-start.3 = (bf16[40,1024]{1,0:T(8,128)(2,1)S(1)}, bf16[40,1024]{1,0:T(8,128)(2,1)S(1)}, u32[]{:S(2)}, u32[]{:S(2)}) collective-permute-start(bf16[40,1024]{1,0:T(8,128)(2,1)S(1)} %pad_maximum_fusion.4), channel_id=1, source_target_pairs={{0,1},{1,0},{2,3},{3,2},{4,5},{5,4},{6,7},{7,6},{8,9},{9,8},{10,11... | collective-permute-start | bytes 245768 | tf_op jit(solution)/shard_map/ppermute | solution.py:256
  81.3 10.0 %collective-permute-start.5 = (bf16[40,1024]{1,0:T(8,128)(2,1)S(1)}, bf16[40,1024]{1,0:T(8,128)(2,1)S(1)}, u32[]{:S(2)}, u32[]{:S(2)}) collective-permute-start(bf16[40,1024]{1,0:T(8,128)(2,1)S(1)} %pad_maximum_fusion.4), channel_id=1, source_target_pairs={{0,35},{1,34},{2,33},{3,32},{4,39},{5,38},{6,37},{7,36},{8,43},{9,... | collective-permute-start | bytes 245768 | tf_op jit(solution)/shard_map/ppermute | solution.py:258
  82.3 9.0 %collective-permute-start.4 = (bf16[40,1024]{1,0:T(8,128)(2,1)S(1)}, bf16[40,1024]{1,0:T(8,128)(2,1)S(1)}, u32[]{:S(2)}, u32[]{:S(2)}) collective-permute-start(bf16[40,1024]{1,0:T(8,128)(2,1)S(1)} %pad_maximum_fusion.3), channel_id=1, source_target_pairs={{0,34},{1,35},{2,32},{3,33},{4,38},{5,39},{6,36},{7,37},{8,42},{9,... | collective-permute-start | bytes 245768 | tf_op jit(solution)/shard_map/ppermute | solution.py:257
  94.8 54.5 %collective-permute-start.6 = (bf16[1280,640]{1,0:T(8,128)(2,1)S(1)}, bf16[1280,640]{1,0:T(8,128)(2,1)}, u32[]{:S(2)}, u32[]{:S(2)}) collective-permute-start(bf16[1280,640]{1,0:T(8,128)(2,1)S(1)} %slice.23), channel_id=1, source_target_pairs={{0,192},{1,193},{2,194},{3,195},{4,196},{5,197},{6,198},{7,199},{8... | collective-permute-start | bytes 4915208 | tf_op jit(solution)/shard_map/ppermute | solution.py:237
  100.6 53.3 %collective-permute-start.7 = (bf16[1280,640]{1,0:T(8,128)(2,1)S(1)}, bf16[1280,640]{1,0:T(8,128)(2,1)}, u32[]{:S(2)}, u32[]{:S(2)}) collective-permute-start(bf16[1280,640]{1,0:T(8,128)(2,1)S(1)} %slice.23), channel_id=1, source_target_pairs={{0,64},{1,65},{2,66},{3,67},{4,68},{5,69},{6,70},{7,71},{8,72},{9,... | collective-permute-start | bytes 4915208 | tf_op jit(solution)/shard_map/ppermute | solution.py:237
  100.6 72.9 %collective-permute-start.10 = (bf16[1280,1280]{1,0:T(8,128)(2,1)}, bf16[1280,1280]{1,0:T(8,128)(2,1)}, u32[]{:S(2)}, u32[]{:S(2)}) collective-permute-start(bf16[1280,1280]{1,0:T(8,128)(2,1)} %all-gather.5.cloned.1.call-done.refs_0_), channel_id=1, source_target_pairs={{0,1},{1,0},{2,3},{3,2},{4,5},{5,4},{6,7},{7,6},{8,9},{9,8},{10,11... | collective-permute-start | bytes 9830408 | tf_op jit(solution)/shard_map/ppermute | solution.py:241
  149.3 22.0 %collective-permute-start.11 = (bf16[1280,640]{1,0:T(8,128)(2,1)}, bf16[1280,640]{1,0:T(8,128)(2,1)}, u32[]{:S(2)}, u32[]{:S(2)}) collective-permute-start(bf16[1280,640]{1,0:T(8,128)(2,1)} %collective-permute-done.6.refs_1_), channel_id=1, source_target_pairs={{0,1},{1,0},{2,3},{3,2},{4,5},{5,4},{6,7},{7,6},{8,9},{9,8},{10,11... | collective-permute-start | bytes 4915208 | tf_op jit(solution)/shard_map/ppermute | solution.py:241
  153.9 19.6 %collective-permute-start.12 = (bf16[1280,640]{1,0:T(8,128)(2,1)}, bf16[1280,640]{1,0:T(8,128)(2,1)}, u32[]{:S(2)}, u32[]{:S(2)}) collective-permute-start(bf16[1280,640]{1,0:T(8,128)(2,1)} %collective-permute-done.7.refs_2_), channel_id=1, source_target_pairs={{0,1},{1,0},{2,3},{3,2},{4,5},{5,4},{6,7},{7,6},{8,9},{9,8},{10,11... | collective-permute-start | bytes 4915208 | tf_op jit(solution)/shard_map/ppermute | solution.py:241
  168.9 47.6 %collective-permute-start.8 = (bf16[1280,512]{1,0:T(8,128)(2,1)}, bf16[1280,512]{1,0:T(8,128)(2,1)}, u32[]{:S(2)}, u32[]{:S(2)}) collective-permute-start(bf16[1280,512]{1,0:T(8,128)(2,1)} %slice.24), channel_id=1, source_target_pairs={{0,192},{1,193},{2,194},{3,195},{4,196},{5,197},{6,198},{7,199},{8... | collective-permute-start | bytes 3932168 | tf_op jit(solution)/shard_map/ppermute | solution.py:237
  171.3 45.2 %collective-permute-start.9 = (bf16[1280,512]{1,0:T(8,128)(2,1)}, bf16[1280,512]{1,0:T(8,128)(2,1)}, u32[]{:S(2)}, u32[]{:S(2)}) collective-permute-start(bf16[1280,512]{1,0:T(8,128)(2,1)} %slice.24), channel_id=1, source_target_pairs={{0,64},{1,65},{2,66},{3,67},{4,68},{5,69},{6,70},{7,71},{8,72},{9,... | collective-permute-start | bytes 3932168 | tf_op jit(solution)/shard_map/ppermute | solution.py:237
  171.3 56.4 %collective-permute-start.13 = (bf16[1280,1024]{1,0:T(8,128)(2,1)}, bf16[1280,1024]{1,0:T(8,128)(2,1)}, u32[]{:S(2)}, u32[]{:S(2)}) collective-permute-start(bf16[1280,1024]{1,0:T(8,128)(2,1)} %all-gather.3.cloned.1.call-done.refs_0_), channel_id=1, source_target_pairs={{0,1},{1,0},{2,3},{3,2},{4,5},{5,4},{6,7},{7,6},{8,9},{9,8},{10,11... | collective-permute-start | bytes 7864328 | tf_op jit(solution)/shard_map/ppermute | solution.py:241
  173.5 1.5 copy-start
  216.5 11.2 %collective-permute-start.14 = (bf16[1280,512]{1,0:T(8,128)(2,1)}, bf16[1280,512]{1,0:T(8,128)(2,1)S(1)}, u32[]{:S(2)}, u32[]{:S(2)}) collective-permute-start(bf16[1280,512]{1,0:T(8,128)(2,1)} %collective-permute-done.8.refs_1_), channel_id=1, source_target_pairs={{0,1},{1,0},{2,3},{3,2},{4,5},{5,4},{6,7},{7,6},{8,9},{9,8},{10,11... | collective-permute-start | bytes 3932168 | tf_op jit(solution)/shard_map/ppermute | solution.py:241
  216.6 11.1 %collective-permute-start.15 = (bf16[1280,512]{1,0:T(8,128)(2,1)}, bf16[1280,512]{1,0:T(8,128)(2,1)S(1)}, u32[]{:S(2)}, u32[]{:S(2)}) collective-permute-start(bf16[1280,512]{1,0:T(8,128)(2,1)} %collective-permute-done.9.refs_2_), channel_id=1, source_target_pairs={{0,1},{1,0},{2,3},{3,2},{4,5},{5,4},{6,7},{7,6},{8,9},{9,8},{10,11... | collective-permute-start | bytes 3932168 | tf_op jit(solution)/shard_map/ppermute | solution.py:241
  218.8 8.9 %collective-permute-start.16 = (bf16[128,1280]{1,0:T(8,128)(2,1)S(1)}, bf16[128,1280]{1,0:T(8,128)(2,1)S(1)}, u32[]{:S(2)}, u32[]{:S(2)}) collective-permute-start(bf16[128,1280]{1,0:T(8,128)(2,1)S(1)} %constant_dynamic-slice_fusion), channel_id=1, source_target_pairs={{0,1},{1,2},{2,3},{3,4},{4,5},{5,6},{6,7},{7,8},{8,9},{9,10},{10,1... | collective-permute-start | bytes 983048 | tf_op jit(solution)/shard_map/ppermute | solution.py:333
  227.7 0.7 copy-start.6
  227.7 1.2 copy-start.4
  228.9 1.1 copy-start.5
Sparse Core Ops, SparseCore 0:
  24.4 68.8 all-gather.4
  95.6 70.7 all-gather.2

commit v3 on v2

--- a/solution.py
+++ b/solution.py
@@ -16,7 +16,6 @@
 HALF = D // 2
 PAIR = 2 * HEAD_DIM
 STEPS = D // (2 * PAIR)
-PIECES = 3
 WIDTHS = (HALF, 512)
 SCALE_LOG2 = 0.125 * math.log2(math.e)
 
@@ -58,7 +57,8 @@
 def layer_kernel(first_block, with_out, scal, lengths, matchings, *refs):
     width_here = WIDTHS[0 if with_out else 1]
     tiles = width_here // PAIR
-    sources, refs = (refs[:PIECES], refs[PIECES : 2 * PIECES]), refs[2 * PIECES :]
+    pieces = 3 if with_out else 4
+    sources, refs = (refs[:pieces], refs[pieces : 2 * pieces]), refs[2 * pieces :]
     if first_block:
         own, refs = refs[0], refs[1:]
     if with_out:
@@ -79,7 +79,9 @@
     def start_tile(half, x_here, index, target, width, sem):
         place = (index // tiles - x_here) % 4
         column = index % tiles * PAIR
-        if place % 2 == 0:
+        if not with_out:
+            piece = place
+        elif place % 2 == 0:
             piece = 0
             column += place // 2 * width_here
         else:
@@ -219,7 +221,7 @@
         grid_spec=pltpu.PrefetchScalarGridSpec(
             num_scalar_prefetch=3,
             grid=(STEPS,),
-            in_specs=[hbm] * (2 * PIECES) + whole,
+            in_specs=[hbm] * (len(mine) + len(yours)) + whole,
             out_specs=pl.BlockSpec((BLK, D), lambda i, *s: (0, 0)),
             scratch_shapes=scratch,
         ),
@@ -289,9 +291,9 @@
         return jnp.pad(columns, ((0, 0), (0, 4 * WIDTHS[1] - 3 * HALF)))
 
     plane_1 = gather_rows(half_1, WIDTHS[1], x, core, y_hi)
-    columns_0, columns_1 = (
+    columns_0, columns_1, far_1 = (
         lax.all_gather(part, "gy", axis=0, tiled=True, axis_index_groups=Z_GROUPS)
-        for part in (plane_0, plane_1)
+        for part in (plane_0, plane_1[:, : WIDTHS[1]], plane_1[:, WIDTHS[1] :])
     )
     spread = lax.all_to_all(spread_in, ALL, 0, 0, tiled=True).reshape(512, HALF)
 
@@ -314,6 +316,7 @@
         axis=1,
     ).reshape(-1)
     chosen = (wanted[:, None] == jnp.arange(512, dtype=jnp.int32)[None, :]).astype(jnp.bfloat16)
+    spread, _ = lax.optimization_barrier((spread, plane_1))
     routed = jnp.dot(chosen, spread, preferred_element_type=jnp.float32).astype(jnp.bfloat16)
     columns_0, _ = lax.optimization_barrier((columns_0, routed))
     collected = lax.all_to_all(routed.reshape(256, 8, HALF), ALL, 0, 0, tiled=True)
@@ -323,7 +326,7 @@
     mine_0 = (columns_0, *near_0)
     yours_0 = other_core(mine_0)
     columns_1, near_0 = lax.optimization_barrier((columns_1, near_0))
-    near_1 = next_to(columns_1[:, : WIDTHS[1]])
+    near_1 = next_to(columns_1)
 
     scal = jnp.stack([here, core, x]).astype(jnp.int32)
     run = functools.partial(layer, scal, lengths, matchings)
@@ -331,10 +334,11 @@
     tail_start = jnp.maximum(lookup(lengths, here) - HALO, 0)
     own_tail = lax.dynamic_slice_in_dim(hidden, tail_start, HALO, 0)
     tail = lax.ppermute(own_tail, ALL, [(i, i + 1) for i in range(255)])
-    far_1 = other_core((columns_1,))
+    here_1 = other_core((columns_1,))
     hidden_1 = run(mine_0, yours_0, (collected,), False, True)
-    near_1, hidden, hidden_1 = lax.optimization_barrier((near_1, hidden, hidden_1))
-    mine_1, yours_1 = (columns_1, *near_1), (*far_1, *other_core(near_1))
+    near_1, far_1, hidden, hidden_1 = lax.optimization_barrier((near_1, far_1, hidden, hidden_1))
+    mine_1 = (columns_1, near_1[0], far_1, near_1[1])
+    yours_1 = (*here_1, *other_core(mine_1[1:]))
     context = run(mine_1, yours_1, (hidden, hidden_1, tail), True, False)
     return hidden, context
 

time: 259 us -> 245 us (0.946)
  starting transfers between devices: 58.6 us -> 51.4 us
  waiting for transfers between devices: 96.6 us -> 93.1 us
    all_to_all x1, waiting for transfers between devices: 28 us -> 17.7 us  [local(): spread = lax.all_to_all(spread_in, ALL, 0, 0, tiled=True).reshape(512, HALF)]
    ppermute x6 -> x7, starting transfers between devices: 16.2 us -> 8.86 us  [other_core(): return tuple((lax.ppermute(piece, ALL, CORE_SWAP) for piece in pieces))]
    ppermute x4, waiting for transfers between devices: 43.5 us -> 48.3 us  [next_to(): return (lax.ppermute(block, ALL, X_DOWN), lax.ppermute(block, ALL, X_UP))]
    all_gather x2 -> x3, waiting for transfers between devices: 9.49 us -> 12.5 us  [local(): lax.all_gather(part, 'gy', axis=0, tiled=True, axis_index_groups=Z_GROUPS)]
  transfers between devices with their start and end apart: 21 -> 23, of which waited for: 7 -> 8; matrix products, arithmetic and copies ran while one was open for 6% -> 6% of each run, Pallas kernels for 16% -> 17%
where the time goes in v3:
time: 245 us; the launch traced here: 242 us
  waiting for transfers between devices  93.1 us (38%)
  Pallas kernels  59.9 us (24%)
  starting transfers between devices  51.4 us (21%)
  local copies, waits for them, and re-layouts  15.4 us (6%)
  between operations  14.7 us (6%)
  other arithmetic  3.72 us (2%)
  matrix products  3.39 us (1%)
    pallas_call x3, Pallas kernels, layer(): pl.pallas_call(functools.partial(layer_kernel, first_block, with_out), gr...  59.9 us
    ppermute x4, waiting for transfers between devices, next_to(): return (lax.ppermute(block, ALL, X_DOWN), lax.ppermute(block, ALL, X_UP))  48.3 us
    all_to_all x1, waiting for transfers between devices, local(): spread = lax.all_to_all(spread_in, ALL, 0, 0, tiled=True).reshape(512, HALF)  17.7 us
    all_to_all x1, starting transfers between devices, local(): spread = lax.all_to_all(spread_in, ALL, 0, 0, tiled=True).reshape(512, HALF)  13.2 us
    all_gather x3, waiting for transfers between devices, local(): lax.all_gather(part, 'gy', axis=0, tiled=True, axis_index_groups=Z_GROUPS)  12.5 us
    ppermute x2, waiting for transfers between devices, gather_rows(): cross = lax.ppermute(keep, ALL, CROSS_SWAP)  10 us
    ppermute x7, starting transfers between devices, other_core(): return tuple((lax.ppermute(piece, ALL, CORE_SWAP) for piece in pieces))  8.86 us
    ppermute x4, starting transfers between devices, next_to(): return (lax.ppermute(block, ALL, X_DOWN), lax.ppermute(block, ALL, X_UP))  7.29 us
  transfers between devices with their start and end apart: 23, of which 8 were waited for; matrix products, arithmetic and copies ran while one was open for 6% of the time, Pallas kernels for 17%

profile of v3, /device:TPU:1, one launch (start us, length us, event | category | flops | bytes accessed | tf_op | source)
XLA Modules:
  0.0 241.7 jit_solution(6084520887588362397)
XLA Ops:
  7.2 0.0 all-gather.6.cloned.1.call-start
  7.2 1.1 slice_bitcast_fusion
  8.3 0.9 pad_maximum_fusion
  9.3 0.3 reshape.154
  9.6 2.6 %dynamic-slice_reduce_fusion.1 = (bf16[40,4,640]{2,1,0:T(4,128)(2,1)S(1)}, bf16[40,4,640]{2,1,0:T(4,128)(2,1)S(1)}) fusion(bf16[40,4,2,640]{3,2,1,0:T(2,128)(2,1)S(1)} %reshape.154, s32[]{:T(128)S(6)} %select_n.85, s32[]{:T(128)S(6)} %select_n.88), kind=kLoop, calls=%fused_computation.7 | loop fusion | bytes 819208 | tf_op jit(solution)/shard_map/jit(dynamic_index_in_dim)/dynamic_slice | solution.py:281
  12.2 3.3 %collective-permute-start = (bf16[40,1280]{1,0:T(8,128)(2,1)S(1)}, bf16[40,1280]{1,0:T(8,128)(2,1)S(1)}, u32[]{:S(2)}, u32[]{:S(2)}) collective-permute-start(bf16[40,1280]{1,0:T(8,128)(2,1)S(1)} %pad_maximum_fusion.2), channel_id=1, source_target_pairs={{0,1},{1,0},{2,3},{3,2},{4,5},{5,4},{6,7},{7,6},{8,9},{9,8},{10,11... | collective-permute-start | bytes 307208 | tf_op jit(solution)/shard_map/ppermute | solution.py:258
  15.5 1.0 collective-permute-start.2
  16.6 1.8 collective-permute-start.1
  18.4 0.1 reshape.157
  18.5 0.0 copy-start.2
  18.5 0.0 copy-start.3
  18.5 0.1 copy.32
  18.7 4.6 %collective-permute-done.1 = bf16[40,1280]{1,0:T(8,128)(2,1)S(1)} collective-permute-done((bf16[40,1280]{1,0:T(8,128)(2,1)S(1)}, bf16[40,1280]{1,0:T(8,128)(2,1)S(1)}, u32[]{:S(2)}, u32[]{:S(2)}) %collective-permute-start.1) | collective-permute-done | bytes 102432 | tf_op jit(solution)/shard_map/ppermute | solution.py:259
  23.3 0.8 maximum_select_fusion
  24.1 0.0 all-gather.6.cloned.1.call-update
  24.2 0.2 select_reduce_fusion.2
  24.4 0.6 fusion.3
  25.0 0.2 select_reduce_fusion
  25.3 1.5 copy.36
  26.8 13.2 %all-to-all-start = ((bf16[256,2,640]{2,1,0:T(2,128)(2,1)}), bf16[256,2,640]{2,1,0:T(2,128)(2,1)S(1)}, u32[]{:S(2)}, u32[]{:S(2)}) async-start(bf16[256,2,640]{2,1,0:T(2,128)(2,1)} %copy.36), calls=%async_computation | async-start | bytes 1310720 | tf_op jit(solution)/shard_map/all_to_all | solution.py:298
  40.1 0.1 copy.35
  40.2 0.1 eq.84
  40.3 0.1 reshape.159
  40.4 2.0 dynamic-slice_reduce_fusion.3
  42.5 2.2 collective-permute-start.3
  44.7 0.9 collective-permute-start.5
  45.7 2.0 collective-permute-start.4
  47.7 5.4 %collective-permute-done.4 = bf16[40,1024]{1,0:T(8,128)(2,1)S(1)} collective-permute-done((bf16[40,1024]{1,0:T(8,128)(2,1)S(1)}, bf16[40,1024]{1,0:T(8,128)(2,1)S(1)}, u32[]{:S(2)}, u32[]{:S(2)}) %collective-permute-start.4) | collective-permute-done | bytes 81952 | tf_op jit(solution)/shard_map/ppermute | solution.py:259
  53.2 0.1 maximum_select_fusion.1
  53.3 17.7 %all-to-all-done = bf16[256,2,640]{2,1,0:T(2,128)(2,1)S(1)} async-done(((bf16[256,2,640]{2,1,0:T(2,128)(2,1)}), bf16[256,2,640]{2,1,0:T(2,128)(2,1)S(1)}, u32[]{:S(2)}, u32[]{:S(2)}) %all-to-all-start) | async-done | bytes 655392 | tf_op jit(solution)/shard_map/all_to_all | solution.py:298
  70.9 0.2 reshape.162
  71.2 3.4 %fusion.1 = bf16[2048,640]{1,0:T(8,128)(2,1)} fusion(bf16[512,640]{1,0:T(8,128)(2,1)S(1)} %reshape.162, s32[2048]{0:T(1024)S(1)} %eq.84), kind=kOutput, calls=%fused_computation.2 | convolution fusion | flops 1344536576 | bytes 3284992 | tf_op jit(solution)/shard_map/dot_general | solution.py:320
  74.6 5.2 %all-to-all-start.1 = ((bf16[256,8,640]{2,1,0:T(8,128)(2,1)}), bf16[256,8,640]{2,1,0:T(8,128)(2,1)S(1)}, u32[]{:S(2)}, u32[]{:S(2)}) async-start(bf16[256,8,640]{2,1,0:T(8,128)(2,1)} %bitcast.38), calls=%async_computation.1 | async-start | bytes 5242880 | tf_op jit(solution)/shard_map/all_to_all | solution.py:322
  79.8 0.0 all-gather.4.cloned.1.call-start
  79.8 12.5 %all-gather.6.cloned.1.call-done.refs_0_ = bf16[1280,1280]{1,0:T(8,128)(2,1)} async-done(((bf16[160,1280]{1,0:T(8,128)(2,1)}), bf16[1280,1280]{1,0:T(8,128)(2,1)}) %all-gather.6.cloned.1.call-update) | async-done | bytes 3276816 | tf_op jit(solution)/shard_map/all_gather | solution.py:295
  92.4 2.8 %slice.27 = bf16[1280,640]{1,0:T(8,128)(2,1)} slice(bf16[1280,1280]{1,0:T(8,128)(2,1)} %all-gather.6.cloned.1.call-done.refs_0_), slice={[0:1280], [0:640]} | slice | bytes 3276800 | tf_op jit(solution)/shard_map/slice | solution.py:325
  95.1 5.8 %collective-permute-start.6 = (bf16[1280,640]{1,0:T(8,128)(2,1)}, bf16[1280,640]{1,0:T(8,128)(2,1)}, u32[]{:S(2)}, u32[]{:S(2)}) collective-permute-start(bf16[1280,640]{1,0:T(8,128)(2,1)} %slice.27), channel_id=1, source_target_pairs={{0,192},{1,193},{2,194},{3,195},{4,196},{5,197},{6,198},{7,199},{8... | collective-permute-start | bytes 4915208 | tf_op jit(solution)/shard_map/ppermute | solution.py:239
  101.0 2.9 %collective-permute-start.10 = (bf16[1280,1280]{1,0:T(8,128)(2,1)}, bf16[1280,1280]{1,0:T(8,128)(2,1)}, u32[]{:S(2)}, u32[]{:S(2)}) collective-permute-start(bf16[1280,1280]{1,0:T(8,128)(2,1)} %all-gather.6.cloned.1.call-done.refs_0_), channel_id=1, source_target_pairs={{0,1},{1,0},{2,3},{3,2},{4,5},{5,4},{6,7},{7,6},{8,9},{9,8},{10,11... | collective-permute-start | bytes 9830408 | tf_op jit(solution)/shard_map/ppermute | solution.py:243
  103.9 0.7 fusion.4
  104.6 0.0 all-gather.4.cloned.1.call-update
  104.7 0.0 all-gather.8.cloned.1.call-start
  104.7 47.0 %collective-permute-done.6.refs_1_ = bf16[1280,640]{1,0:T(8,128)(2,1)} collective-permute-done((bf16[1280,640]{1,0:T(8,128)(2,1)}, bf16[1280,640]{1,0:T(8,128)(2,1)}, u32[]{:S(2)}, u32[]{:S(2)}) %collective-permute-start.6) | collective-permute-done | bytes 1638432 | tf_op jit(solution)/shard_map/ppermute | solution.py:239
  151.7 2.4 collective-permute-start.11
  154.1 1.3 collective-permute-done.7.refs_2_
  155.4 2.3 collective-permute-start.12
  157.6 0.0 all-gather.8.cloned.1.call-update
  157.7 0.6 pad_add_fusion.scal
  158.3 1.5 collective-permute-start.9
  159.8 0.6 collective-permute-start.13
  160.3 0.8 collective-permute-done.12.refs_5_
  161.1 0.8 copy-done
  161.9 20.8 %shard_map.69.refs_9_ = bf16[256,1280]{1,0:T(8,128)(2,1)} custom-call(s32[3]{0:T(128)} %pad_add_fusion.scal, s32[256]{0:T(256)} %lengths.5, s32[2,256]{1,0:T(2,128)} %matchings.5, bf16[1280,1280]{1,0:T(8,128)(2,1)} %all-gather.6.cloned.1.call-done.refs_0_, bf16[1280,640]{1,0:T(8,128)(2,1)} %collective-permute-done.6.refs_1_, ...), custom_call_target="tpu_custom_call" | custom-call | flops 8000000000 | bytes 14000000 | tf_op jit(solution)/shard_map/pallas_call | solution.py:219
  182.7 20.6 %shard_map.68.refs_8_ = bf16[256,1280]{1,0:T(8,128)(2,1)} custom-call(s32[3]{0:T(128)} %pad_add_fusion.scal, s32[256]{0:T(256)} %lengths.5, s32[2,256]{1,0:T(2,128)} %matchings.5, bf16[1280,1280]{1,0:T(8,128)(2,1)} %all-gather.6.cloned.1.call-done.refs_0_, bf16[1280,640]{1,0:T(8,128)(2,1)} %collective-permute-done.6.refs_1_, ...), custom_call_target="tpu_custom_call" | custom-call | flops 8000000000 | bytes 14000000 | tf_op jit(solution)/shard_map/pallas_call | solution.py:219
  203.3 0.0 all-gather.8.cloned.1.call-done.refs_2_
  203.3 0.1 collective-permute-start.14
  203.5 0.5 collective-permute-start.15
  203.9 0.1 collective-permute-start.16
  204.6 1.1 constant_dynamic-slice_fusion
  205.7 5.5 %collective-permute-start.17 = (bf16[128,1280]{1,0:T(8,128)(2,1)S(1)}, bf16[128,1280]{1,0:T(8,128)(2,1)S(1)}, u32[]{:S(2)}, u32[]{:S(2)}) collective-permute-start(bf16[128,1280]{1,0:T(8,128)(2,1)S(1)} %constant_dynamic-slice_fusion), channel_id=1, source_target_pairs={{0,1},{1,2},{2,3},{3,4},{4,5},{5,6},{6,7},{7,8},{8,9},{9,10},{10,1... | collective-permute-start | bytes 983048 | tf_op jit(solution)/shard_map/ppermute | solution.py:336
  211.2 3.7 %collective-permute-done.17.refs_10_ = bf16[128,1280]{1,0:T(8,128)(2,1)S(1)} collective-permute-done((bf16[128,1280]{1,0:T(8,128)(2,1)S(1)}, bf16[128,1280]{1,0:T(8,128)(2,1)S(1)}, u32[]{:S(2)}, u32[]{:S(2)}) %collective-permute-start.17) | collective-permute-done | bytes 327712 | tf_op jit(solution)/shard_map/ppermute | solution.py:336
  215.0 0.7 copy-done.6
  215.7 0.4 copy-done.4
  216.1 0.4 copy-done.5
  216.5 18.6 %shard_map.70 = bf16[256,1280]{1,0:T(8,128)(2,1)} custom-call(s32[3]{0:T(128)} %pad_add_fusion.scal, s32[256]{0:T(256)} %lengths.5, s32[2,256]{1,0:T(2,128)} %matchings.5, bf16[1280,512]{1,0:T(8,128)(2,1)} %all-gather.4.cloned.1.call-done.refs_0_, bf16[1280,512]{1,0:T(8,128)(2,1)} %collective-permute-done.8.refs_1_, ...), custom_call_target="tpu_custom_call" | custom-call | flops 8000000000 | bytes 14000000 | tf_op jit(solution)/shard_map/pallas_call | solution.py:219
  (48 shorter events, 0.5 us)
Async XLA Ops:
  7.2 85.2 %all-gather.6.cloned.1.call-start = ((), (), s32[]{:S(2)}) async-start(), calls=%async_computation.3 | async-start | bytes 3686400 | tf_op jit(solution)/shard_map/all_gather | solution.py:295
  9.6 8.8 %copy-start.1 = (bf16[256,1280]{1,0:T(8,128)(2,1)S(1)}, bf16[256,1280]{1,0:T(8,128)(2,1)}, u32[]{:S(2)}) copy-start(bf16[256,1280]{1,0:T(8,128)(2,1)} %refs_6_.1) | copy-start | bytes 1966084
  12.2 6.4 %collective-permute-start = (bf16[40,1280]{1,0:T(8,128)(2,1)S(1)}, bf16[40,1280]{1,0:T(8,128)(2,1)S(1)}, u32[]{:S(2)}, u32[]{:S(2)}) collective-permute-start(bf16[40,1280]{1,0:T(8,128)(2,1)S(1)} %pad_maximum_fusion.2), channel_id=1, source_target_pairs={{0,1},{1,0},{2,3},{3,2},{4,5},{5,4},{6,7},{7,6},{8,9},{9,8},{10,11... | collective-permute-start | bytes 307208 | tf_op jit(solution)/shard_map/ppermute | solution.py:258
  15.5 7.7 %collective-permute-start.2 = (bf16[40,1280]{1,0:T(8,128)(2,1)S(1)}, bf16[40,1280]{1,0:T(8,128)(2,1)S(1)}, u32[]{:S(2)}, u32[]{:S(2)}) collective-permute-start(bf16[40,1280]{1,0:T(8,128)(2,1)S(1)} %pad_maximum_fusion.2), channel_id=1, source_target_pairs={{0,35},{1,34},{2,33},{3,32},{4,39},{5,38},{6,37},{7,36},{8,43},{9,... | collective-permute-start | bytes 307208 | tf_op jit(solution)/shard_map/ppermute | solution.py:260
  16.6 6.7 %collective-permute-start.1 = (bf16[40,1280]{1,0:T(8,128)(2,1)S(1)}, bf16[40,1280]{1,0:T(8,128)(2,1)S(1)}, u32[]{:S(2)}, u32[]{:S(2)}) collective-permute-start(bf16[40,1280]{1,0:T(8,128)(2,1)S(1)} %pad_maximum_fusion.1), channel_id=1, source_target_pairs={{0,34},{1,35},{2,32},{3,33},{4,38},{5,39},{6,36},{7,37},{8,42},{9,... | collective-permute-start | bytes 307208 | tf_op jit(solution)/shard_map/ppermute | solution.py:259
  18.5 5.7 %copy-start.2 = (s32[2,256]{1,0:T(2,128)S(1)}, s32[2,256]{1,0:T(2,128)}, u32[]{:S(2)}) copy-start(s32[2,256]{1,0:T(2,128)} %matchings.5) | copy-start | bytes 6148
  18.5 5.9 %copy-start.3 = (s32[256]{0:T(256)S(1)}, s32[256]{0:T(256)}, u32[]{:S(2)}) copy-start(s32[256]{0:T(256)} %lengths.5) | copy-start | bytes 3076
  26.8 44.1 %all-to-all-start = ((bf16[256,2,640]{2,1,0:T(2,128)(2,1)}), bf16[256,2,640]{2,1,0:T(2,128)(2,1)S(1)}, u32[]{:S(2)}, u32[]{:S(2)}) async-start(bf16[256,2,640]{2,1,0:T(2,128)(2,1)} %copy.36), calls=%async_computation | async-start | bytes 1310720 | tf_op jit(solution)/shard_map/all_to_all | solution.py:298
  42.5 5.2 %collective-permute-start.3 = (bf16[40,1024]{1,0:T(8,128)(2,1)S(1)}, bf16[40,1024]{1,0:T(8,128)(2,1)S(1)}, u32[]{:S(2)}, u32[]{:S(2)}) collective-permute-start(bf16[40,1024]{1,0:T(8,128)(2,1)S(1)} %pad_maximum_fusion.4), channel_id=1, source_target_pairs={{0,1},{1,0},{2,3},{3,2},{4,5},{5,4},{6,7},{7,6},{8,9},{9,8},{10,11... | collective-permute-start | bytes 245768 | tf_op jit(solution)/shard_map/ppermute | solution.py:258
  44.7 8.5 %collective-permute-start.5 = (bf16[40,1024]{1,0:T(8,128)(2,1)S(1)}, bf16[40,1024]{1,0:T(8,128)(2,1)S(1)}, u32[]{:S(2)}, u32[]{:S(2)}) collective-permute-start(bf16[40,1024]{1,0:T(8,128)(2,1)S(1)} %pad_maximum_fusion.4), channel_id=1, source_target_pairs={{0,35},{1,34},{2,33},{3,32},{4,39},{5,38},{6,37},{7,36},{8,43},{9,... | collective-permute-start | bytes 245768 | tf_op jit(solution)/shard_map/ppermute | solution.py:260
  45.7 7.5 %collective-permute-start.4 = (bf16[40,1024]{1,0:T(8,128)(2,1)S(1)}, bf16[40,1024]{1,0:T(8,128)(2,1)S(1)}, u32[]{:S(2)}, u32[]{:S(2)}) collective-permute-start(bf16[40,1024]{1,0:T(8,128)(2,1)S(1)} %pad_maximum_fusion.3), channel_id=1, source_target_pairs={{0,34},{1,35},{2,32},{3,33},{4,38},{5,39},{6,36},{7,37},{8,42},{9,... | collective-permute-start | bytes 245768 | tf_op jit(solution)/shard_map/ppermute | solution.py:259
  74.6 85.8 %all-to-all-start.1 = ((bf16[256,8,640]{2,1,0:T(8,128)(2,1)}), bf16[256,8,640]{2,1,0:T(8,128)(2,1)S(1)}, u32[]{:S(2)}, u32[]{:S(2)}) async-start(bf16[256,8,640]{2,1,0:T(8,128)(2,1)} %bitcast.38), calls=%async_computation.1 | async-start | bytes 5242880 | tf_op jit(solution)/shard_map/all_to_all | solution.py:322
  79.8 78.5 %all-gather.4.cloned.1.call-start = ((), (), s32[]{:S(2)}) async-start(), calls=%async_computation.2 | async-start | bytes 1474560 | tf_op jit(solution)/shard_map/all_gather | solution.py:295
  95.1 56.5 %collective-permute-start.6 = (bf16[1280,640]{1,0:T(8,128)(2,1)}, bf16[1280,640]{1,0:T(8,128)(2,1)}, u32[]{:S(2)}, u32[]{:S(2)}) collective-permute-start(bf16[1280,640]{1,0:T(8,128)(2,1)} %slice.27), channel_id=1, source_target_pairs={{0,192},{1,193},{2,194},{3,195},{4,196},{5,197},{6,198},{7,199},{8... | collective-permute-start | bytes 4915208 | tf_op jit(solution)/shard_map/ppermute | solution.py:239
  101.0 54.4 %collective-permute-start.7 = (bf16[1280,640]{1,0:T(8,128)(2,1)}, bf16[1280,640]{1,0:T(8,128)(2,1)}, u32[]{:S(2)}, u32[]{:S(2)}) collective-permute-start(bf16[1280,640]{1,0:T(8,128)(2,1)} %slice.27), channel_id=1, source_target_pairs={{0,64},{1,65},{2,66},{3,67},{4,68},{5,69},{6,70},{7,71},{8,72},{9,... | collective-permute-start | bytes 4915208 | tf_op jit(solution)/shard_map/ppermute | solution.py:239
  101.0 60.1 %collective-permute-start.10 = (bf16[1280,1280]{1,0:T(8,128)(2,1)}, bf16[1280,1280]{1,0:T(8,128)(2,1)}, u32[]{:S(2)}, u32[]{:S(2)}) collective-permute-start(bf16[1280,1280]{1,0:T(8,128)(2,1)} %all-gather.6.cloned.1.call-done.refs_0_), channel_id=1, source_target_pairs={{0,1},{1,0},{2,3},{3,2},{4,5},{5,4},{6,7},{7,6},{8,9},{9,8},{10,11... | collective-permute-start | bytes 9830408 | tf_op jit(solution)/shard_map/ppermute | solution.py:243
  104.7 98.7 %all-gather.8.cloned.1.call-start = ((), (), s32[]{:S(2)}) async-start(), calls=%async_computation.4 | async-start | bytes 1474560 | tf_op jit(solution)/shard_map/all_gather | solution.py:295
  151.7 8.1 %collective-permute-start.11 = (bf16[1280,640]{1,0:T(8,128)(2,1)}, bf16[1280,640]{1,0:T(8,128)(2,1)}, u32[]{:S(2)}, u32[]{:S(2)}) collective-permute-start(bf16[1280,640]{1,0:T(8,128)(2,1)} %collective-permute-done.6.refs_1_), channel_id=1, source_target_pairs={{0,1},{1,0},{2,3},{3,2},{4,5},{5,4},{6,7},{7,6},{8,9},{9,8},{10,11... | collective-permute-start | bytes 4915208 | tf_op jit(solution)/shard_map/ppermute | solution.py:243
  155.4 5.7 %collective-permute-start.12 = (bf16[1280,640]{1,0:T(8,128)(2,1)}, bf16[1280,640]{1,0:T(8,128)(2,1)}, u32[]{:S(2)}, u32[]{:S(2)}) collective-permute-start(bf16[1280,640]{1,0:T(8,128)(2,1)} %collective-permute-done.7.refs_2_), channel_id=1, source_target_pairs={{0,1},{1,0},{2,3},{3,2},{4,5},{5,4},{6,7},{7,6},{8,9},{9,8},{10,11... | collective-permute-start | bytes 4915208 | tf_op jit(solution)/shard_map/ppermute | solution.py:243
  158.3 45.0 %collective-permute-start.8 = (bf16[1280,512]{1,0:T(8,128)(2,1)}, bf16[1280,512]{1,0:T(8,128)(2,1)}, u32[]{:S(2)}, u32[]{:S(2)}) collective-permute-start(bf16[1280,512]{1,0:T(8,128)(2,1)} %all-gather.4.cloned.1.call-done.refs_0_), channel_id=1, source_target_pairs={{0,192},{1,193},{2,194},{3,195},{4,196},{5,197},{6,198},{7,199},{8... | collective-permute-start | bytes 3932168 | tf_op jit(solution)/shard_map/ppermute | solution.py:239
  158.3 45.0 %collective-permute-start.9 = (bf16[1280,512]{1,0:T(8,128)(2,1)}, bf16[1280,512]{1,0:T(8,128)(2,1)}, u32[]{:S(2)}, u32[]{:S(2)}) collective-permute-start(bf16[1280,512]{1,0:T(8,128)(2,1)} %all-gather.4.cloned.1.call-done.refs_0_), channel_id=1, source_target_pairs={{0,64},{1,65},{2,66},{3,67},{4,68},{5,69},{6,70},{7,71},{8,72},{9,... | collective-permute-start | bytes 3932168 | tf_op jit(solution)/shard_map/ppermute | solution.py:239
  159.8 51.4 %collective-permute-start.13 = (bf16[1280,512]{1,0:T(8,128)(2,1)}, bf16[1280,512]{1,0:T(8,128)(2,1)}, u32[]{:S(2)}, u32[]{:S(2)}) collective-permute-start(bf16[1280,512]{1,0:T(8,128)(2,1)} %all-gather.4.cloned.1.call-done.refs_0_), channel_id=1, source_target_pairs={{0,1},{1,0},{2,3},{3,2},{4,5},{5,4},{6,7},{7,6},{8,9},{9,8},{10,11... | collective-permute-start | bytes 3932168 | tf_op jit(solution)/shard_map/ppermute | solution.py:243
  160.3 1.6 copy-start
  203.3 11.6 %collective-permute-start.14 = (bf16[1280,512]{1,0:T(8,128)(2,1)}, bf16[1280,512]{1,0:T(8,128)(2,1)S(1)}, u32[]{:S(2)}, u32[]{:S(2)}) collective-permute-start(bf16[1280,512]{1,0:T(8,128)(2,1)} %collective-permute-done.8.refs_1_), channel_id=1, source_target_pairs={{0,1},{1,0},{2,3},{3,2},{4,5},{5,4},{6,7},{7,6},{8,9},{9,8},{10,11... | collective-permute-start | bytes 3932168 | tf_op jit(solution)/shard_map/ppermute | solution.py:243
  203.5 11.5 %collective-permute-start.15 = (bf16[1280,512]{1,0:T(8,128)(2,1)}, bf16[1280,512]{1,0:T(8,128)(2,1)S(1)}, u32[]{:S(2)}, u32[]{:S(2)}) collective-permute-start(bf16[1280,512]{1,0:T(8,128)(2,1)} %all-gather.8.cloned.1.call-done.refs_2_), channel_id=1, source_target_pairs={{0,1},{1,0},{2,3},{3,2},{4,5},{5,4},{6,7},{7,6},{8,9},{9,8},{10,11... | collective-permute-start | bytes 3932168 | tf_op jit(solution)/shard_map/ppermute | solution.py:243
  203.9 11.0 %collective-permute-start.16 = (bf16[1280,512]{1,0:T(8,128)(2,1)}, bf16[1280,512]{1,0:T(8,128)(2,1)}, u32[]{:S(2)}, u32[]{:S(2)}) collective-permute-start(bf16[1280,512]{1,0:T(8,128)(2,1)} %collective-permute-done.9.refs_3_), channel_id=1, source_target_pairs={{0,1},{1,0},{2,3},{3,2},{4,5},{5,4},{6,7},{7,6},{8,9},{9,8},{10,11... | collective-permute-start | bytes 3932168 | tf_op jit(solution)/shard_map/ppermute | solution.py:243
  205.7 9.3 %collective-permute-start.17 = (bf16[128,1280]{1,0:T(8,128)(2,1)S(1)}, bf16[128,1280]{1,0:T(8,128)(2,1)S(1)}, u32[]{:S(2)}, u32[]{:S(2)}) collective-permute-start(bf16[128,1280]{1,0:T(8,128)(2,1)S(1)} %constant_dynamic-slice_fusion), channel_id=1, source_target_pairs={{0,1},{1,2},{2,3},{3,4},{4,5},{5,6},{6,7},{7,8},{8,9},{9,10},{10,1... | collective-permute-start | bytes 983048 | tf_op jit(solution)/shard_map/ppermute | solution.py:336
  215.0 0.7 copy-start.6
  215.0 1.2 copy-start.4
  215.0 1.6 copy-start.5
Sparse Core Ops, SparseCore 0:
  24.3 68.0 all-gather.5
  104.8 50.9 all-gather.3
  158.1 35.8 all-gather.7
